TPU v7x, 256 devices: a whole 4x4x8 slice. The times are simulated.
256 devices in a mesh: field: 16 (over z_hi, y), space: 16 (over z_lo, x, core).
Axes of the slice: x: 4, y: 4, z: 8 (z_hi: 4, z_lo: 2; z = z_hi * 2 + z_lo), core: 2. Of those that a mesh axis runs over, the one named last changes fastest.
Arguments:
- fields: float32 [3, 64, 1024, 1024], P(None, 'field', 'space'), may hold values from -6 to 6
- increments: float32 [3, 64, 1024, 1024], P(None, 'field', 'space'), may hold values from -6 to 6
- velocity: float32 [2, 1024, 1024], P(None, 'space', 'field'), may hold values from -25 to 25
- geometry: int32 [1024, 1024], P('space'), may hold values from 0 to 1, as said below
Outputs:
- fields_new: float32 [3, 64, 1024, 1024], P(None, 'field', 'space')
- velocity_new: float32 [2, 1024, 1024], P(None, 'space', 'field')
Inputs may be any that keep to these rules, and one draw needn't show every extreme that they name: `geometry`: the walls occupy a band of rows at each side of the grid, the same width on both, over all columns from some column to the last.
All inputs are finite; a program needn't handle non-finite values. Where the computation divides by a largest or mean magnitude, that divisor is 1e-20 or more.
Results may differ from a plain program's by a relative error of at most 0.0003.
Values sent between devices are 32-bit elements; how exact they have to be, the bound alone decides.
A program may use at most 64 MiB of HBM per device.

v0:
```python
import jax
import jax.numpy as jnp
from jax import lax
from jax.sharding import PartitionSpec as P

ITERS = 8


COURANT = 0.5
SPEED_EPS = 1e-06
RELAX = 0.5
MODULUS = 2.0
BETA = 0.5
VISCOSITY = 1.0
PENALTY = 20.0
LOWER = BETA
UPPER = BETA + PENALTY + 8.0 * VISCOSITY


def extended(block, sides, width):
    for axis, dim in sides:
        count = lax.axis_size(axis)
        forward = [(i, i + 1) for i in range(count - 1)]
        backward = [(target, source) for source, target in forward]
        low = lax.ppermute(
            lax.slice_in_dim(block, block.shape[dim] - width, None, axis=dim), axis, forward
        )
        high = lax.ppermute(lax.slice_in_dim(block, 0, width, axis=dim), axis, backward)
        block = jnp.concatenate([low, block, high], axis=dim)
    return block


def neighbour(values, axis, offset):
    widths = [(0, 0)] * values.ndim
    widths[axis] = (1, 1)
    padded = jnp.pad(values, widths)
    return lax.slice_in_dim(padded, 1 + offset, 1 + offset + values.shape[axis], axis=axis)


def centred(values, axis):
    return 0.5 * (neighbour(values, axis, 1) - neighbour(values, axis, -1))


def evolve(
    deviation, above, below, noise, flow_down, flow_across, gradients, time_step, noise_scale
):
    last = deviation.ndim - 1
    left = neighbour(deviation, last, -1)
    right = neighbour(deviation, last, 1)
    advected = (
        jnp.maximum(flow_down, 0.0) * (deviation - above)
        + jnp.minimum(flow_down, 0.0) * (below - deviation)
        + jnp.maximum(flow_across, 0.0) * (deviation - left)
        + jnp.minimum(flow_across, 0.0) * (right - deviation)
    )
    down_down, down_across, across_down, across_across = gradients
    comp_down = deviation[0] + 1.0
    comp_shear = deviation[1]
    comp_across = deviation[2] + 1.0
    stretch = jnp.stack(
        [
            2.0 * (down_down * comp_down + down_across * comp_shear),
            down_down * comp_shear
            + down_across * comp_across
            + comp_down * across_down
            + comp_shear * across_across,
            2.0 * (across_down * comp_shear + across_across * comp_across),
        ]
    )
    return deviation + time_step * (stretch - advected - deviation / RELAX) + noise_scale * noise


def bordered_divergence(bordered):

    def along_rows(values):
        return 0.5 * (values[2:, 1:-1] - values[:-2, 1:-1])

    def along_cols(values):
        return 0.5 * (values[1:-1, 2:] - values[1:-1, :-2])

    return jnp.stack(
        [
            along_rows(bordered[0]) + along_cols(bordered[1]),
            along_rows(bordered[1]) + along_cols(bordered[2]),
        ]
    )


def chebyshev(start, source, apply):
    centre = 0.5 * (UPPER + LOWER)
    radius = 0.5 * (UPPER - LOWER)
    sigma = centre / radius
    rho = 1.0 / sigma
    solution = start
    residual = source - apply(start)
    direction = residual / centre
    for index in range(ITERS):
        solution = solution + direction
        if index + 1 < ITERS:
            residual = residual - apply(direction)
            rho_next = 1.0 / (2.0 * sigma - rho)
            direction = rho_next * rho * direction + 2.0 * rho_next / radius * residual
            rho = rho_next
    return solution


def per_device(fields, increments, velocity, geometry):
    tile_cols = velocity.shape[2]
    col_start = lax.axis_index("field") * tile_cols
    total_fields = fields.shape[1] * lax.axis_size("field")
    strip_velocity = lax.all_gather(velocity, "field", axis=2, tiled=True)
    speed_max = lax.pmax(jnp.max(jnp.abs(strip_velocity)), "space")
    time_step = COURANT / (speed_max + SPEED_EPS)
    noise_scale = jnp.sqrt(time_step / RELAX)
    velocity_rim = extended(strip_velocity, (("space", 1),), 1)
    flow_down = strip_velocity[0]
    flow_across = strip_velocity[1]
    gradients = (
        0.5 * (velocity_rim[0, 2:] - velocity_rim[0, :-2]),
        centred(flow_down, 1),
        0.5 * (velocity_rim[1, 2:] - velocity_rim[1, :-2]),
        centred(flow_across, 1),
    )
    identity = jnp.array([1.0, 0.0, 1.0], jnp.float32).reshape(3, 1, 1, 1)
    deviation = fields - identity
    field_rim = extended(deviation, (("space", 2),), 1)
    new_deviation = evolve(
        deviation,
        field_rim[:, :, :-2],
        field_rim[:, :, 2:],
        increments,
        flow_down,
        flow_across,
        gradients,
        time_step,
        noise_scale,
    )
    fields_new = new_deviation + identity
    mask_values = geometry.astype(jnp.float32)
    partial_stress = MODULUS / total_fields * jnp.sum(new_deviation * mask_values, axis=1)
    whole_stress = lax.psum(partial_stress, "field")
    tile_stress = lax.dynamic_slice_in_dim(whole_stress, col_start, tile_cols, 2)
    bordered = extended(tile_stress, (("field", 2), ("space", 1)), 1)
    force = bordered_divergence(bordered)
    tile_mask = lax.dynamic_slice_in_dim(mask_values, col_start, tile_cols, 1)
    wall = PENALTY * (1.0 - tile_mask)

    def apply(values):
        bordered_values = extended(values, (("field", 2), ("space", 1)), 1)
        beside = (
            bordered_values[:, 2:, 1:-1]
            + bordered_values[:, :-2, 1:-1]
            + bordered_values[:, 1:-1, 2:]
            + bordered_values[:, 1:-1, :-2]
        )
        return (BETA + 4.0 * VISCOSITY + wall) * values - VISCOSITY * beside

    source = BETA * velocity + force
    velocity_new = chebyshev(velocity, source, apply)
    return (fields_new, velocity_new)


def solution(mesh):
    placed = (
        P(None, "field", "space", None),
        P(None, "field", "space", None),
        P(None, "space", "field"),
        P("space", None),
    )
    return jax.shard_map(
        per_device,
        mesh=mesh,
        in_specs=placed,
        out_specs=(P(None, "field", "space", None), P(None, "space", "field")),
        check_vma=False,
    )
```

profile of v0, /device:TPU:120, one launch (start us, length us, event | category | flops | bytes accessed | tf_op | source)
XLA Modules:
  0.0 490.4 jit_solution(10432283550157151135)
XLA Ops:
  8.1 46.2 %all_gather.3 = f32[2,64,1024]{1,0,2:T(2,128)S(1)} all-gather(f32[2,64,64]{1,0,2:T(2,128)S(1)} %copy.31), channel_id=1, replica_groups=mesh['field'=16,'space'=16] {'field'}, dimensions={2}, use_global_device_ids=true | all-gather | bytes 557056 | tf_op jit(solution)/shard_map/all_gather | solution.py:111
  55.9 1.9 collective-permute-start
  58.3 2.5 collective-permute-start.1
  60.9 2.3 broadcast_add_fusion
  64.9 3.0 collective-permute-start.2
  69.7 4.6 collective-permute-start.3
  74.3 27.8 %pmax.7 = f32[]{:T(128)} all-reduce(f32[]{:T(128)} %abs_reduce_fusion), channel_id=1, replica_groups=mesh['field'=16,'space'=16] {'space'}, use_global_device_ids=true, to_apply=%region_1.0 | all-reduce | flops 1 | bytes 8 | tf_op jit(solution)/shard_map/pmax | solution.py:112
  104.7 8.2 %fusion.20 = (f32[1,64,1024]{1,0,2:T(1,128)}, f32[1,64,1024]{1,0,2:T(1,128)}, f32[1,64,1024]{1,0,2:T(1,128)}, f32[1,64,1024]{1,0,2:T(1,128)}) fusion(f32[2,64,1024]{1,0,2:T(2,128)S(1)} %all_gather.3, f32[2,1,1024]{1,0,2:T(2,128)S(1)} %copy.35, f32[2,1,1024]{1,0,2:T(2,128)S(1)} %copy.33), kind=kLoop, calls=%fused_computation.39 | loop fusion | flops 524288 | bytes 5242880 | tf_op jit(solution)/shard_map/mul | solution.py:119
  116.1 1.9 copy.36
  118.1 1.9 copy.38
  123.5 5.7 %multiply_reduce_fusion = (f32[3,64,1024]{2,1,0:T(8,128)S(1)}, f32[3,4,64,1024]{3,2,1,0:T(8,128)}) fusion(f32[64,1024]{1,0:T(8,128)S(1)} %copy-done.6, f32[3,4,64,1024]{3,2,1,0:T(8,128)S(1)} %copy-done.3, f32[]{:T(128)S(6)} %sqrt.3, f32[3,4,64,1024]{3,2,1,0:T(8,128)S(1)} %copy-done.1, f32[64,1024]{1,0:T(8,128)S(1)} %get-tuple-element.36, ...), kind=kLoop, calls=%fused_computation.20 | loop fusion | flops 18677760 | bytes 14778376 | tf_op jit(solution)/shard_map/reduce_sum | solution.py:140
  130.4 8.3 %collective-permute-start.8 = (f32[2,64,1]{2,1,0:T(8,128)S(1)}, f32[2,64,1]{2,1,0:T(8,128)S(1)}, u32[]{:S(2)}, u32[]{:S(2)}) collective-permute-start(f32[2,64,1]{2,1,0:T(8,128)S(1)} %get-tuple-element.71), channel_id=1, source_target_pairs={{0,16},{16,32},{32,48},{48,64},{64,80},{80,96},{96,112},{112,128},... | collective-permute-start | bytes 1544 | tf_op jit(solution)/shard_map/ppermute | solution.py:25
  138.7 1.9 collective-permute-start.9
  141.5 156.1 %all-reduce.5.cloned.1.call-done = f32[3,64,1024]{2,1,0:T(8,128)} async-done(((f32[3,64,1024]{2,1,0:T(8,128)}), f32[3,64,1024]{2,1,0:T(8,128)}) %all-reduce.5.cloned.1.call-update) | async-done | bytes 786448 | tf_op jit(solution)/shard_map/psum | solution.py:141
  298.6 3.8 collective-permute-start.4
  302.4 2.0 collective-permute-start.5
  305.5 7.8 %collective-permute-done.5 = f32[3,64,1]{2,1,0:T(8,128)S(1)} collective-permute-done((f32[3,64,1]{2,1,0:T(8,128)S(1)}, f32[3,64,1]{2,1,0:T(8,128)S(1)}, u32[]{:S(2)}, u32[]{:S(2)}) %collective-permute-start.5) | collective-permute-done | bytes 800 | tf_op jit(solution)/shard_map/ppermute | solution.py:28
  313.3 1.9 collective-permute-start.6
  315.3 5.8 %collective-permute-start.7 = (f32[3,1,66]{2,1,0:T(1,128)S(1)}, f32[3,1,66]{2,1,0:T(1,128)S(1)}, u32[]{:S(2)}, u32[]{:S(2)}) collective-permute-start(f32[3,1,66]{2,1,0:T(1,128)S(1)} %get-tuple-element.32), channel_id=1, source_target_pairs={{1,0},{2,1},{3,2},{4,3},{5,4},{6,5},{7,6},{8,7},{9,8},{10,9},{11,1... | collective-permute-start | bytes 2384 | tf_op jit(solution)/shard_map/ppermute | solution.py:28
  321.1 2.7 collective-permute-start.10
  323.8 1.9 collective-permute-start.11
  326.1 4.7 collective-permute-done.11
  331.1 1.9 collective-permute-start.12
  333.0 3.9 collective-permute-start.13
  337.3 6.1 %collective-permute-done.13 = f32[2,64,1]{2,1,0:T(8,128)S(1)} collective-permute-done((f32[2,64,1]{2,1,0:T(8,128)S(1)}, f32[2,64,1]{2,1,0:T(8,128)S(1)}, u32[]{:S(2)}, u32[]{:S(2)}) %collective-permute-start.13) | collective-permute-done | bytes 544 | tf_op jit(solution)/shard_map/ppermute | solution.py:28
  343.5 1.9 collective-permute-start.14
  345.4 2.4 collective-permute-start.15
  347.8 4.6 collective-permute-done.15
  352.7 1.9 collective-permute-start.16
  354.6 4.1 collective-permute-start.17
  358.9 6.2 %collective-permute-done.17 = f32[2,64,1]{2,1,0:T(8,128)S(1)} collective-permute-done((f32[2,64,1]{2,1,0:T(8,128)S(1)}, f32[2,64,1]{2,1,0:T(8,128)S(1)}, u32[]{:S(2)}, u32[]{:S(2)}) %collective-permute-start.17) | collective-permute-done | bytes 544 | tf_op jit(solution)/shard_map/ppermute | solution.py:28
  365.1 1.9 collective-permute-start.18
  367.0 2.4 collective-permute-start.19
  369.4 4.6 collective-permute-done.19
  374.3 1.9 collective-permute-start.20
  376.2 3.9 collective-permute-start.21
  380.5 6.8 %collective-permute-done.21 = f32[2,64,1]{2,1,0:T(8,128)S(1)} collective-permute-done((f32[2,64,1]{2,1,0:T(8,128)S(1)}, f32[2,64,1]{2,1,0:T(8,128)S(1)}, u32[]{:S(2)}, u32[]{:S(2)}) %collective-permute-start.21) | collective-permute-done | bytes 544 | tf_op jit(solution)/shard_map/ppermute | solution.py:28
  387.3 1.9 collective-permute-start.22
  389.2 2.4 collective-permute-start.23
  391.7 4.6 collective-permute-done.23
  396.5 1.9 collective-permute-start.24
  398.4 3.9 collective-permute-start.25
  402.7 6.1 %collective-permute-done.25 = f32[2,64,1]{2,1,0:T(8,128)S(1)} collective-permute-done((f32[2,64,1]{2,1,0:T(8,128)S(1)}, f32[2,64,1]{2,1,0:T(8,128)S(1)}, u32[]{:S(2)}, u32[]{:S(2)}) %collective-permute-start.25) | collective-permute-done | bytes 544 | tf_op jit(solution)/shard_map/ppermute | solution.py:28
  408.9 1.9 collective-permute-start.26
  410.8 2.4 collective-permute-start.27
  413.2 4.6 collective-permute-done.27
  418.1 1.9 collective-permute-start.28
  420.0 3.9 collective-permute-start.29
  424.2 6.1 %collective-permute-done.29 = f32[2,64,1]{2,1,0:T(8,128)S(1)} collective-permute-done((f32[2,64,1]{2,1,0:T(8,128)S(1)}, f32[2,64,1]{2,1,0:T(8,128)S(1)}, u32[]{:S(2)}, u32[]{:S(2)}) %collective-permute-start.29) | collective-permute-done | bytes 544 | tf_op jit(solution)/shard_map/ppermute | solution.py:28
  430.5 1.9 collective-permute-start.30
  432.4 2.4 collective-permute-start.31
  434.8 4.6 collective-permute-done.31
  439.7 1.9 collective-permute-start.32
  441.6 3.9 collective-permute-start.33
  445.8 6.1 %collective-permute-done.33 = f32[2,64,1]{2,1,0:T(8,128)S(1)} collective-permute-done((f32[2,64,1]{2,1,0:T(8,128)S(1)}, f32[2,64,1]{2,1,0:T(8,128)S(1)}, u32[]{:S(2)}, u32[]{:S(2)}) %collective-permute-start.33) | collective-permute-done | bytes 544 | tf_op jit(solution)/shard_map/ppermute | solution.py:28
  452.1 1.9 collective-permute-start.34
  454.0 2.4 collective-permute-start.35
  456.4 4.6 collective-permute-done.35
  461.3 1.9 collective-permute-start.36
  463.2 3.9 collective-permute-start.37
  467.4 6.1 %collective-permute-done.37 = f32[2,64,1]{2,1,0:T(8,128)S(1)} collective-permute-done((f32[2,64,1]{2,1,0:T(8,128)S(1)}, f32[2,64,1]{2,1,0:T(8,128)S(1)}, u32[]{:S(2)}, u32[]{:S(2)}) %collective-permute-start.37) | collective-permute-done | bytes 544 | tf_op jit(solution)/shard_map/ppermute | solution.py:28
  475.6 2.4 collective-permute-start.39
  478.0 2.1 broadcast_add_fusion.1
  480.1 2.5 collective-permute-done.39
  (93 shorter events, 26.7 us)
Async XLA Ops:
  7.2 290.4 %all-reduce.5.cloned.1.call-start = ((), (), s32[]{:S(2)}) async-start(), calls=%async_computation | async-start | bytes 1572864 | tf_op jit(solution)/shard_map/psum | solution.py:141
  54.3 6.6 %copy-start.9 = (f32[3]{0:T(128)S(1)}, f32[3]{0:T(128)}, u32[]{:S(2)}) copy-start(f32[3]{0:T(128)} %constant.81) | copy-start | bytes 40
  55.9 47.6 %collective-permute-start = (f32[2,1,1024]{2,0,1:T(2,128)S(1)}, f32[2,1,1024]{2,0,1:T(2,128)S(1)}, u32[]{:S(2)}, u32[]{:S(2)}) collective-permute-start(f32[2,1,1024]{2,0,1:T(2,128)S(1)} %copy.32), channel_id=1, source_target_pairs={{1,0},{2,1},{3,2},{4,3},{5,4},{6,5},{7,6},{8,7},{9,8},{10,9},{11,1... | collective-permute-start | bytes 24584 | tf_op jit(solution)/shard_map/ppermute | solution.py:28
  58.3 44.5 %copy-start.7 = (s32[64,1024]{1,0:T(8,128)S(1)}, s32[64,1024]{1,0:T(8,128)}, u32[]{:S(2)}) copy-start(s32[64,1024]{1,0:T(8,128)} %param.8) | copy-start | bytes 786436
  58.3 45.8 %collective-permute-start.1 = (f32[2,1,1024]{2,0,1:T(2,128)S(1)}, f32[2,1,1024]{2,0,1:T(2,128)S(1)}, u32[]{:S(2)}, u32[]{:S(2)}) collective-permute-start(f32[2,1,1024]{2,0,1:T(2,128)S(1)} %copy.34), channel_id=1, source_target_pairs={{0,1},{1,2},{2,3},{3,4},{4,5},{5,6},{6,7},{7,8},{8,9},{9,10},{10,1... | collective-permute-start | bytes 24584 | tf_op jit(solution)/shard_map/ppermute | solution.py:25
  63.2 1.7 copy-start
  64.9 58.4 %collective-permute-start.2 = (f32[3,4,1,1024]{3,2,1,0:T(1,128)S(1)}, f32[3,4,1,1024]{3,2,1,0:T(1,128)}, u32[]{:S(2)}, u32[]{:S(2)}) collective-permute-start(f32[3,4,1,1024]{3,2,1,0:T(1,128)S(1)} %get-tuple-element.23), channel_id=1, source_target_pairs={{0,1},{1,2},{2,3},{3,4},{4,5},{5,6},{6,7},{7,8},{8,9},{9,10},{10,1... | collective-permute-start | bytes 147464 | tf_op jit(solution)/shard_map/ppermute | solution.py:25
  69.7 53.7 %collective-permute-start.3 = (f32[3,4,1,1024]{3,2,1,0:T(1,128)S(1)}, f32[3,4,1,1024]{3,2,1,0:T(1,128)}, u32[]{:S(2)}, u32[]{:S(2)}) collective-permute-start(f32[3,4,1,1024]{3,2,1,0:T(1,128)S(1)} %get-tuple-element.24), channel_id=1, source_target_pairs={{1,0},{2,1},{3,2},{4,3},{5,4},{6,5},{7,6},{8,7},{9,8},{10,9},{11,1... | collective-permute-start | bytes 147464 | tf_op jit(solution)/shard_map/ppermute | solution.py:28
  112.9 8.5 %copy-start.1 = (f32[3,4,64,1024]{3,2,1,0:T(8,128)S(1)}, f32[3,4,64,1024]{3,2,1,0:T(8,128)}, u32[]{:S(2)}) copy-start(f32[3,4,64,1024]{3,2,1,0:T(8,128)} %copy-done) | copy-start | bytes 9437188
  121.4 1.8 copy-start.4
  121.4 2.1 copy-start.3
  121.4 2.1 copy-start.6
  123.5 6.7 %copy-start.5 = (f32[2,64,64]{2,1,0:T(8,128)S(1)}, f32[2,64,64]{2,1,0:T(8,128)}, u32[]{:S(2)}) copy-start(f32[2,64,64]{2,1,0:T(8,128)} %param.7) | copy-start | bytes 98308
  130.4 190.7 %collective-permute-start.8 = (f32[2,64,1]{2,1,0:T(8,128)S(1)}, f32[2,64,1]{2,1,0:T(8,128)S(1)}, u32[]{:S(2)}, u32[]{:S(2)}) collective-permute-start(f32[2,64,1]{2,1,0:T(8,128)S(1)} %get-tuple-element.71), channel_id=1, source_target_pairs={{0,16},{16,32},{32,48},{48,64},{64,80},{80,96},{96,112},{112,128},... | collective-permute-start | bytes 1544 | tf_op jit(solution)/shard_map/ppermute | solution.py:25
  138.7 182.3 %collective-permute-start.9 = (f32[2,64,1]{2,1,0:T(8,128)S(1)}, f32[2,64,1]{2,1,0:T(8,128)S(1)}, u32[]{:S(2)}, u32[]{:S(2)}) collective-permute-start(f32[2,64,1]{2,1,0:T(8,128)S(1)} %get-tuple-element.70), channel_id=1, source_target_pairs={{16,0},{32,16},{48,32},{64,48},{80,64},{96,80},{112,96},{128,112},... | collective-permute-start | bytes 1544 | tf_op jit(solution)/shard_map/ppermute | solution.py:28
  298.6 6.9 %collective-permute-start.4 = (f32[3,64,1]{2,1,0:T(8,128)S(1)}, f32[3,64,1]{2,1,0:T(8,128)S(1)}, u32[]{:S(2)}, u32[]{:S(2)}) collective-permute-start(f32[3,64,1]{2,1,0:T(8,128)S(1)} %get-tuple-element.29), channel_id=1, source_target_pairs={{0,16},{16,32},{32,48},{48,64},{64,80},{80,96},{96,112},{112,128},... | collective-permute-start | bytes 2312 | tf_op jit(solution)/shard_map/ppermute | solution.py:25
  302.4 10.8 %collective-permute-start.5 = (f32[3,64,1]{2,1,0:T(8,128)S(1)}, f32[3,64,1]{2,1,0:T(8,128)S(1)}, u32[]{:S(2)}, u32[]{:S(2)}) collective-permute-start(f32[3,64,1]{2,1,0:T(8,128)S(1)} %get-tuple-element.30), channel_id=1, source_target_pairs={{16,0},{32,16},{48,32},{64,48},{80,64},{96,80},{112,96},{128,112},... | collective-permute-start | bytes 2312 | tf_op jit(solution)/shard_map/ppermute | solution.py:28
  313.3 12.4 %collective-permute-start.6 = (f32[3,1,66]{2,1,0:T(1,128)S(1)}, f32[3,1,66]{2,1,0:T(1,128)S(1)}, u32[]{:S(2)}, u32[]{:S(2)}) collective-permute-start(f32[3,1,66]{2,1,0:T(1,128)S(1)} %get-tuple-element.31), channel_id=1, source_target_pairs={{0,1},{1,2},{2,3},{3,4},{4,5},{5,6},{6,7},{7,8},{8,9},{9,10},{10,1... | collective-permute-start | bytes 2384 | tf_op jit(solution)/shard_map/ppermute | solution.py:25
  315.3 10.5 %collective-permute-start.7 = (f32[3,1,66]{2,1,0:T(1,128)S(1)}, f32[3,1,66]{2,1,0:T(1,128)S(1)}, u32[]{:S(2)}, u32[]{:S(2)}) collective-permute-start(f32[3,1,66]{2,1,0:T(1,128)S(1)} %get-tuple-element.32), channel_id=1, source_target_pairs={{1,0},{2,1},{3,2},{4,3},{5,4},{6,5},{7,6},{8,7},{9,8},{10,9},{11,1... | collective-permute-start | bytes 2384 | tf_op jit(solution)/shard_map/ppermute | solution.py:28
  321.1 5.0 %collective-permute-start.10 = (f32[2,1,66]{2,1,0:T(1,128)S(1)}, f32[2,1,66]{2,1,0:T(1,128)S(1)}, u32[]{:S(2)}, u32[]{:S(2)}) collective-permute-start(f32[2,1,66]{2,1,0:T(1,128)S(1)} %get-tuple-element.51), channel_id=1, source_target_pairs={{1,0},{2,1},{3,2},{4,3},{5,4},{6,5},{7,6},{8,7},{9,8},{10,9},{11,1... | collective-permute-start | bytes 1592 | tf_op jit(solution)/shard_map/ppermute | solution.py:28
  323.8 7.0 %collective-permute-start.11 = (f32[2,1,66]{2,1,0:T(1,128)S(1)}, f32[2,1,66]{2,1,0:T(1,128)S(1)}, u32[]{:S(2)}, u32[]{:S(2)}) collective-permute-start(f32[2,1,66]{2,1,0:T(1,128)S(1)} %get-tuple-element.52), channel_id=1, source_target_pairs={{0,1},{1,2},{2,3},{3,4},{4,5},{5,6},{6,7},{7,8},{8,9},{9,10},{10,1... | collective-permute-start | bytes 1592 | tf_op jit(solution)/shard_map/ppermute | solution.py:25
  326.1 151.9 %copy-start.2 = (f32[3,4,64,1024]{3,2,1,0:T(8,128)S(1)}, f32[3,4,64,1024]{3,2,1,0:T(8,128)}, u32[]{:S(2)}) copy-start(f32[3,4,64,1024]{3,2,1,0:T(8,128)} %get-tuple-element.17) | copy-start | bytes 9437188
  326.1 151.9 %copy-start.8 = (f32[3]{0:T(128)S(1)}, f32[3]{0:T(128)}, u32[]{:S(2)}) copy-start(f32[3]{0:T(128)} %constant.72.clone) | copy-start | bytes 40
  331.1 6.2 %collective-permute-start.12 = (f32[2,64,1]{2,1,0:T(8,128)S(1)}, f32[2,64,1]{2,1,0:T(8,128)S(1)}, u32[]{:S(2)}, u32[]{:S(2)}) collective-permute-start(f32[2,64,1]{2,1,0:T(8,128)S(1)} %get-tuple-element.69), channel_id=1, source_target_pairs={{0,16},{16,32},{32,48},{48,64},{64,80},{80,96},{96,112},{112,128},... | collective-permute-start | bytes 1544 | tf_op jit(solution)/shard_map/ppermute | solution.py:25
  333.0 10.4 %collective-permute-start.13 = (f32[2,64,1]{2,1,0:T(8,128)S(1)}, f32[2,64,1]{2,1,0:T(8,128)S(1)}, u32[]{:S(2)}, u32[]{:S(2)}) collective-permute-start(f32[2,64,1]{2,1,0:T(8,128)S(1)} %get-tuple-element.68), channel_id=1, source_target_pairs={{16,0},{32,16},{48,32},{64,48},{80,64},{96,80},{112,96},{128,112},... | collective-permute-start | bytes 1544 | tf_op jit(solution)/shard_map/ppermute | solution.py:28
  343.5 4.3 collective-permute-start.14
  345.4 7.0 %collective-permute-start.15 = (f32[2,1,66]{2,1,0:T(1,128)S(1)}, f32[2,1,66]{2,1,0:T(1,128)S(1)}, u32[]{:S(2)}, u32[]{:S(2)}) collective-permute-start(f32[2,1,66]{2,1,0:T(1,128)S(1)} %get-tuple-element.50), channel_id=1, source_target_pairs={{0,1},{1,2},{2,3},{3,4},{4,5},{5,6},{6,7},{7,8},{8,9},{9,10},{10,1... | collective-permute-start | bytes 1592 | tf_op jit(solution)/shard_map/ppermute | solution.py:25
  352.7 6.2 %collective-permute-start.16 = (f32[2,64,1]{2,1,0:T(8,128)S(1)}, f32[2,64,1]{2,1,0:T(8,128)S(1)}, u32[]{:S(2)}, u32[]{:S(2)}) collective-permute-start(f32[2,64,1]{2,1,0:T(8,128)S(1)} %get-tuple-element.67), channel_id=1, source_target_pairs={{0,16},{16,32},{32,48},{48,64},{64,80},{80,96},{96,112},{112,128},... | collective-permute-start | bytes 1544 | tf_op jit(solution)/shard_map/ppermute | solution.py:25
  354.6 10.4 %collective-permute-start.17 = (f32[2,64,1]{2,1,0:T(8,128)S(1)}, f32[2,64,1]{2,1,0:T(8,128)S(1)}, u32[]{:S(2)}, u32[]{:S(2)}) collective-permute-start(f32[2,64,1]{2,1,0:T(8,128)S(1)} %get-tuple-element.66), channel_id=1, source_target_pairs={{16,0},{32,16},{48,32},{64,48},{80,64},{96,80},{112,96},{128,112},... | collective-permute-start | bytes 1544 | tf_op jit(solution)/shard_map/ppermute | solution.py:28
  365.1 4.3 collective-permute-start.18
  367.0 7.0 %collective-permute-start.19 = (f32[2,1,66]{2,1,0:T(1,128)S(1)}, f32[2,1,66]{2,1,0:T(1,128)S(1)}, u32[]{:S(2)}, u32[]{:S(2)}) collective-permute-start(f32[2,1,66]{2,1,0:T(1,128)S(1)} %get-tuple-element.48), channel_id=1, source_target_pairs={{0,1},{1,2},{2,3},{3,4},{4,5},{5,6},{6,7},{7,8},{8,9},{9,10},{10,1... | collective-permute-start | bytes 1592 | tf_op jit(solution)/shard_map/ppermute | solution.py:25
  374.3 6.2 %collective-permute-start.20 = (f32[2,64,1]{2,1,0:T(8,128)S(1)}, f32[2,64,1]{2,1,0:T(8,128)S(1)}, u32[]{:S(2)}, u32[]{:S(2)}) collective-permute-start(f32[2,64,1]{2,1,0:T(8,128)S(1)} %get-tuple-element.65), channel_id=1, source_target_pairs={{0,16},{16,32},{32,48},{48,64},{64,80},{80,96},{96,112},{112,128},... | collective-permute-start | bytes 1544 | tf_op jit(solution)/shard_map/ppermute | solution.py:25
  376.2 11.0 %collective-permute-start.21 = (f32[2,64,1]{2,1,0:T(8,128)S(1)}, f32[2,64,1]{2,1,0:T(8,128)S(1)}, u32[]{:S(2)}, u32[]{:S(2)}) collective-permute-start(f32[2,64,1]{2,1,0:T(8,128)S(1)} %get-tuple-element.64), channel_id=1, source_target_pairs={{16,0},{32,16},{48,32},{64,48},{80,64},{96,80},{112,96},{128,112},... | collective-permute-start | bytes 1544 | tf_op jit(solution)/shard_map/ppermute | solution.py:28
  387.3 4.3 collective-permute-start.22
  389.2 7.0 %collective-permute-start.23 = (f32[2,1,66]{2,1,0:T(1,128)S(1)}, f32[2,1,66]{2,1,0:T(1,128)S(1)}, u32[]{:S(2)}, u32[]{:S(2)}) collective-permute-start(f32[2,1,66]{2,1,0:T(1,128)S(1)} %get-tuple-element.46), channel_id=1, source_target_pairs={{0,1},{1,2},{2,3},{3,4},{4,5},{5,6},{6,7},{7,8},{8,9},{9,10},{10,1... | collective-permute-start | bytes 1592 | tf_op jit(solution)/shard_map/ppermute | solution.py:25
  396.5 6.2 %collective-permute-start.24 = (f32[2,64,1]{2,1,0:T(8,128)S(1)}, f32[2,64,1]{2,1,0:T(8,128)S(1)}, u32[]{:S(2)}, u32[]{:S(2)}) collective-permute-start(f32[2,64,1]{2,1,0:T(8,128)S(1)} %get-tuple-element.63), channel_id=1, source_target_pairs={{0,16},{16,32},{32,48},{48,64},{64,80},{80,96},{96,112},{112,128},... | collective-permute-start | bytes 1544 | tf_op jit(solution)/shard_map/ppermute | solution.py:25
  398.4 10.4 %collective-permute-start.25 = (f32[2,64,1]{2,1,0:T(8,128)S(1)}, f32[2,64,1]{2,1,0:T(8,128)S(1)}, u32[]{:S(2)}, u32[]{:S(2)}) collective-permute-start(f32[2,64,1]{2,1,0:T(8,128)S(1)} %get-tuple-element.62), channel_id=1, source_target_pairs={{16,0},{32,16},{48,32},{64,48},{80,64},{96,80},{112,96},{128,112},... | collective-permute-start | bytes 1544 | tf_op jit(solution)/shard_map/ppermute | solution.py:28
  408.9 4.3 collective-permute-start.26
  410.8 7.0 %collective-permute-start.27 = (f32[2,1,66]{2,1,0:T(1,128)S(1)}, f32[2,1,66]{2,1,0:T(1,128)S(1)}, u32[]{:S(2)}, u32[]{:S(2)}) collective-permute-start(f32[2,1,66]{2,1,0:T(1,128)S(1)} %get-tuple-element.44), channel_id=1, source_target_pairs={{0,1},{1,2},{2,3},{3,4},{4,5},{5,6},{6,7},{7,8},{8,9},{9,10},{10,1... | collective-permute-start | bytes 1592 | tf_op jit(solution)/shard_map/ppermute | solution.py:25
  418.1 6.2 %collective-permute-start.28 = (f32[2,64,1]{2,1,0:T(8,128)S(1)}, f32[2,64,1]{2,1,0:T(8,128)S(1)}, u32[]{:S(2)}, u32[]{:S(2)}) collective-permute-start(f32[2,64,1]{2,1,0:T(8,128)S(1)} %get-tuple-element.61), channel_id=1, source_target_pairs={{0,16},{16,32},{32,48},{48,64},{64,80},{80,96},{96,112},{112,128},... | collective-permute-start | bytes 1544 | tf_op jit(solution)/shard_map/ppermute | solution.py:25
  420.0 10.4 %collective-permute-start.29 = (f32[2,64,1]{2,1,0:T(8,128)S(1)}, f32[2,64,1]{2,1,0:T(8,128)S(1)}, u32[]{:S(2)}, u32[]{:S(2)}) collective-permute-start(f32[2,64,1]{2,1,0:T(8,128)S(1)} %get-tuple-element.60), channel_id=1, source_target_pairs={{16,0},{32,16},{48,32},{64,48},{80,64},{96,80},{112,96},{128,112},... | collective-permute-start | bytes 1544 | tf_op jit(solution)/shard_map/ppermute | solution.py:28
  430.5 4.3 collective-permute-start.30
  432.4 7.0 %collective-permute-start.31 = (f32[2,1,66]{2,1,0:T(1,128)S(1)}, f32[2,1,66]{2,1,0:T(1,128)S(1)}, u32[]{:S(2)}, u32[]{:S(2)}) collective-permute-start(f32[2,1,66]{2,1,0:T(1,128)S(1)} %get-tuple-element.42), channel_id=1, source_target_pairs={{0,1},{1,2},{2,3},{3,4},{4,5},{5,6},{6,7},{7,8},{8,9},{9,10},{10,1... | collective-permute-start | bytes 1592 | tf_op jit(solution)/shard_map/ppermute | solution.py:25
  439.7 6.2 %collective-permute-start.32 = (f32[2,64,1]{2,1,0:T(8,128)S(1)}, f32[2,64,1]{2,1,0:T(8,128)S(1)}, u32[]{:S(2)}, u32[]{:S(2)}) collective-permute-start(f32[2,64,1]{2,1,0:T(8,128)S(1)} %get-tuple-element.59), channel_id=1, source_target_pairs={{0,16},{16,32},{32,48},{48,64},{64,80},{80,96},{96,112},{112,128},... | collective-permute-start | bytes 1544 | tf_op jit(solution)/shard_map/ppermute | solution.py:25
  441.6 10.4 %collective-permute-start.33 = (f32[2,64,1]{2,1,0:T(8,128)S(1)}, f32[2,64,1]{2,1,0:T(8,128)S(1)}, u32[]{:S(2)}, u32[]{:S(2)}) collective-permute-start(f32[2,64,1]{2,1,0:T(8,128)S(1)} %get-tuple-element.58), channel_id=1, source_target_pairs={{16,0},{32,16},{48,32},{64,48},{80,64},{96,80},{112,96},{128,112},... | collective-permute-start | bytes 1544 | tf_op jit(solution)/shard_map/ppermute | solution.py:28
  452.1 4.3 collective-permute-start.34
  454.0 7.0 %collective-permute-start.35 = (f32[2,1,66]{2,1,0:T(1,128)S(1)}, f32[2,1,66]{2,1,0:T(1,128)S(1)}, u32[]{:S(2)}, u32[]{:S(2)}) collective-permute-start(f32[2,1,66]{2,1,0:T(1,128)S(1)} %get-tuple-element.40), channel_id=1, source_target_pairs={{0,1},{1,2},{2,3},{3,4},{4,5},{5,6},{6,7},{7,8},{8,9},{9,10},{10,1... | collective-permute-start | bytes 1592 | tf_op jit(solution)/shard_map/ppermute | solution.py:25
  461.3 6.2 %collective-permute-start.36 = (f32[2,64,1]{2,1,0:T(8,128)S(1)}, f32[2,64,1]{2,1,0:T(8,128)S(1)}, u32[]{:S(2)}, u32[]{:S(2)}) collective-permute-start(f32[2,64,1]{2,1,0:T(8,128)S(1)} %get-tuple-element.57), channel_id=1, source_target_pairs={{0,16},{16,32},{32,48},{48,64},{64,80},{80,96},{96,112},{112,128},... | collective-permute-start | bytes 1544 | tf_op jit(solution)/shard_map/ppermute | solution.py:25
  463.2 10.4 %collective-permute-start.37 = (f32[2,64,1]{2,1,0:T(8,128)S(1)}, f32[2,64,1]{2,1,0:T(8,128)S(1)}, u32[]{:S(2)}, u32[]{:S(2)}) collective-permute-start(f32[2,64,1]{2,1,0:T(8,128)S(1)} %get-tuple-element.56), channel_id=1, source_target_pairs={{16,0},{32,16},{48,32},{64,48},{80,64},{96,80},{112,96},{128,112},... | collective-permute-start | bytes 1544 | tf_op jit(solution)/shard_map/ppermute | solution.py:28
  473.6 6.4 %collective-permute-start.38 = (f32[2,1,66]{2,1,0:T(1,128)S(1)}, f32[2,1,66]{2,1,0:T(1,128)S(1)}, u32[]{:S(2)}, u32[]{:S(2)}) collective-permute-start(f32[2,1,66]{2,1,0:T(1,128)S(1)} %get-tuple-element.37), channel_id=1, source_target_pairs={{1,0},{2,1},{3,2},{4,3},{5,4},{6,5},{7,6},{8,7},{9,8},{10,9},{11,1... | collective-permute-start | bytes 1592 | tf_op jit(solution)/shard_map/ppermute | solution.py:28
  475.6 7.0 %collective-permute-start.39 = (f32[2,1,66]{2,1,0:T(1,128)S(1)}, f32[2,1,66]{2,1,0:T(1,128)S(1)}, u32[]{:S(2)}, u32[]{:S(2)}) collective-permute-start(f32[2,1,66]{2,1,0:T(1,128)S(1)} %get-tuple-element.38), channel_id=1, source_target_pairs={{0,1},{1,2},{2,3},{3,4},{4,5},{5,6},{6,7},{7,8},{8,9},{9,10},{10,1... | collective-permute-start | bytes 1592 | tf_op jit(solution)/shard_map/ppermute | solution.py:25
Sparse Core Ops, SparseCore 0:
  130.4 167.1 all-reduce.4
where the time goes:
time: 492 us; the launch traced here: 490 us
  waiting for transfers between devices  244 us (50%)
  starting transfers between devices  112 us (23%)
  blocking collectives  74 us (15%)
  other arithmetic  29 us (6%)
  local copies, waits for them, and re-layouts  15.9 us (3%)
  between operations  15.5 us (3%)
    psum x1, waiting for transfers between devices, per_device(): whole_stress = lax.psum(partial_stress, 'field')  156 us
    ppermute x20, starting transfers between devices, extended(): lax.ppermute(lax.slice_in_dim(block, 0, width, axis=dim), axis, backward)  60 us
    ppermute x20, starting transfers between devices, extended(): lax.ppermute(lax.slice_in_dim(block, block.shape[dim] - width, None, axis...  51.8 us
    ppermute x20, waiting for transfers between devices, extended(): lax.ppermute(lax.slice_in_dim(block, 0, width, axis=dim), axis, backward)  51.5 us
    all_gather x1, blocking collectives, per_device(): strip_velocity = lax.all_gather(velocity, 'field', axis=2, tiled=True)  46.2 us
    ppermute x20, waiting for transfers between devices, extended(): lax.ppermute(lax.slice_in_dim(block, block.shape[dim] - width, None, axis...  36.6 us
    pmax x1, blocking collectives, per_device(): speed_max = lax.pmax(jnp.max(jnp.abs(strip_velocity)), 'space')  27.8 us
  transfers between devices with their start and end apart: 41, of which 24 were waited for; matrix products, arithmetic and copies ran while one was open for 6% of the time, Pallas kernels for 0%

commit v1 on v0

v1 whole, which is shorter than its diff:
```python
import functools

import jax
import jax.numpy as jnp
from jax import lax
from jax.experimental import pallas as pl
from jax.experimental.pallas import tpu as pltpu
from jax.sharding import PartitionSpec as P

ITERS = 8
COURANT = 0.5
SPEED_EPS = 1e-06
RELAX = 0.5
MODULUS = 2.0
BETA = 0.5
VISCOSITY = 1.0
PENALTY = 20.0
LOWER = BETA
UPPER = BETA + PENALTY + 8.0 * VISCOSITY

MESH = pl.DeviceIdType.MESH
F32 = jnp.float32
LANES = 128
ROWS = 64
HALO = 8
TALL = ROWS + 2 * HALO
TILE = 64
TILES = 16
COLS = 8
FIELDS = 64
LOCAL = 4
RING = 4
PACKED = 72
SPLIT = 40
STRESS = 96
HALF = STRESS // 2
ORDER = (2, 1, 3, 0)


def slots():
    names = [("max", d) for d in range(1, 16)]
    names += [(n, d) for n in ("vrow", "frow", "own", "ownrow", "vcorner", "edge") for d in (0, 1)]
    names += [(n, o) for n in ("z", "zrow") for o in (1, 2, 3)]
    names += [("y", o, d) for o in (1, 2, 3) for d in (0, 1)]
    names += [("relay", o, d) for o in range(4) for d in (0, 1)]
    names += [(n, j, d) for n in ("half", "whole") for j in range(4) for d in (0, 1)]
    names += [("reduced", j) for j in range(3)]
    names += [("corner", a, b) for a in (0, 1) for b in (0, 1)]
    names += [("srow", d) for d in (0, 1)]
    return {name: at for at, name in enumerate(names)}


SLOTS = slots()


def kernel(
    fields, noise, velocity, geometry, fields_out, velocity_out,
    X, N, V, G, U, PG, M_own, M_all, VR_out, VR_in, FR_out, FR_in, VC_out, VC_in,
    Q, H_in, W_in, Z_in, T, E, B, B_in, E_in, local_sem, out_sem, send_sem, recv_sem,
):
    f = lax.axis_index("field")
    s = lax.axis_index("space")
    zh = f // RING
    y = f % RING
    right = zh * RING + (y + 1) % RING
    left = zh * RING + (y + RING - 1) % RING
    f_up, f_down = (f + 1) % TILES, (f + TILES - 1) % TILES
    s_up, s_down = (s + 1) % TILES, (s + TILES - 1) % TILES

    def z_peer(o):
        return (zh + o) % RING * RING + y

    def z_source(o):
        return (zh + RING - o) % RING * RING + y

    started = []

    def send(name, source, target, to_f, to_s):
        copy = pltpu.make_async_remote_copy(
            src_ref=source,
            dst_ref=target,
            send_sem=send_sem.at[SLOTS[name]],
            recv_sem=recv_sem.at[SLOTS[name]],
            device_id=(to_f, to_s),
            device_id_type=MESH,
        )
        copy.start()
        started.append(copy)

    def arrive(name, landed):
        pltpu.make_async_copy(landed, landed, recv_sem.at[SLOTS[name]]).wait()

    load_v = pltpu.make_async_copy(velocity, V, local_sem.at[0])
    load_v.start()
    load_g = pltpu.make_async_copy(geometry, G, local_sem.at[1])
    load_g.start()
    load_x, load_n = [], []
    for t in range(COLS):
        columns = slice(t * LANES, (t + 1) * LANES)
        load_x.append(
            pltpu.make_async_copy(
                fields.at[:, :, :, columns],
                X.at[:, :, t + 1, HALO : HALO + ROWS, :],
                local_sem.at[2 + t],
            )
        )
    for t in range(COLS):
        columns = slice(t * LANES, (t + 1) * LANES)
        load_n.append(
            pltpu.make_async_copy(
                noise.at[:, :, :, columns], N.at[:, :, t], local_sem.at[2 + COLS + t]
            )
        )
    for copy in load_x + load_n:
        copy.start()

    barrier = pltpu.get_barrier_semaphore()
    partners = [(f, (s + d) % TILES) for d in range(1, TILES)]
    partners += [(right, s), (left, s)]
    partners += [(z_peer(o), s) for o in (1, 2, 3)]
    partners += [(f_up, s), (f_down, s)]
    partners += [(a, b) for a in (f_up, f_down) for b in (s_up, s_down)]
    for partner in partners:
        pl.semaphore_signal(barrier, inc=1, device_id=partner, device_id_type=MESH)

    lane = lax.broadcasted_iota(jnp.int32, (8, LANES), 1)
    low = lane < TILE

    load_v.wait()
    own = jnp.concatenate([V[0], V[1]], axis=1)
    PG[f, 0:ROWS, :] = own
    M_own[...] = jnp.max(jnp.abs(own).reshape(ROWS // 8, 8, LANES), axis=0)
    VR_out[0, 0:8, :] = own[ROWS - 8 :]
    VR_out[1, 0:8, :] = own[0:8]

    load_g.wait()
    half = f % 2
    t_own = f // 2

    def walls(rows):
        def block(t):
            at = pl.multiple_of(jnp.clip(t, 0, COLS - 1) * LANES, LANES)
            return G[rows, pl.ds(at, LANES)].astype(F32)

        before, here, after = block(t_own - 1), block(t_own), block(t_own + 1)
        count = here.shape[0]
        at = lax.broadcasted_iota(jnp.int32, (count, LANES), 1)
        even = pltpu.roll(jnp.where(at < 120, here, before), HALO, axis=1)
        odd = pltpu.roll(jnp.where(at < HALO, after, here), HALO + TILE, axis=1)
        return jnp.where(half == 0, even, odd)

    VR_out[0, 8:16, :] = walls(slice(ROWS - 8, ROWS))
    VR_out[1, 8:16, :] = walls(slice(0, 8))

    pl.semaphore_wait(barrier, len(partners))

    main = PG.at[f, 0:ROWS]
    send(("own", 0), main, main, right, s)
    send(("own", 1), main, main, left, s)
    for o in (2, 1, 3):
        send(("z", o), main, main, z_peer(o), s)
    for d in range(1, TILES):
        send(("max", d), M_own, M_all.at[d], f, (s + d) % TILES)
    send(("vrow", 0), VR_out.at[0], VR_in.at[0], f, s_up)
    send(("vrow", 1), VR_out.at[1], VR_in.at[1], f, s_down)

    for copy in load_x:
        copy.wait()
    for c in range(3):
        for e in range(LOCAL):
            for t in range(COLS):
                FR_out[0, c * LOCAL + e, t : t + 1, :] = X[c, e, t + 1, HALO + ROWS - 1 : HALO + ROWS, :]
                FR_out[1, c * LOCAL + e, t : t + 1, :] = X[c, e, t + 1, HALO : HALO + 1, :]
    send(("frow", 0), FR_out.at[0], FR_in.at[0], f, s_up)
    send(("frow", 1), FR_out.at[1], FR_in.at[1], f, s_down)

    first, last = s == 0, s == TILES - 1
    for d in (0, 1):
        arrive(("vrow", d), VR_in.at[d])
    speed = M_own[...]
    for d in range(1, TILES):
        arrive(("max", d), M_all.at[d])
        speed = jnp.maximum(speed, M_all[d])
    speed = jnp.max(speed, axis=0, keepdims=True)
    above = jnp.where(first, 0.0, VR_in[0, 7:8, :])
    below = jnp.where(last, 0.0, VR_in[1, 0:1, :])
    PG[f, ROWS : ROWS + 1, :] = above
    PG[f, ROWS + 1 : ROWS + 2, :] = below
    PG[f, ROWS + 2 : PACKED, :] = jnp.broadcast_to(speed, (PACKED - ROWS - 2, LANES))
    rim = PG.at[f, ROWS:PACKED]
    send(("ownrow", 0), rim, rim, right, s)
    send(("ownrow", 1), rim, rim, left, s)
    for o in (2, 1, 3):
        send(("zrow", o), rim, rim, z_peer(o), s)
    VC_out[0:8, :] = VR_in[0, 0:8, :]
    VC_out[8:16, :] = VR_in[1, 0:8, :]
    send(("vcorner", 0), VC_out, VC_in.at[0], f_up, s)
    send(("vcorner", 1), VC_out, VC_in.at[1], f_down, s)

    def ring_tile(o, step):
        return (zh + RING - o) % RING * RING + (y + step) % RING

    def forward(o):
        tile = z_source(o)
        arrive(("z", o), PG.at[tile, 0:ROWS])
        arrive(("zrow", o), PG.at[tile, ROWS:PACKED])
        send(("y", o, 0), PG.at[tile], PG.at[tile], right, s)
        send(("y", o, 1), PG.at[tile], PG.at[tile], left, s)

    def relay(o):
        for d, step in ((0, RING - 1), (1, 1)):
            tile = ring_tile(o, step)
            if o == 0:
                arrive(("own", d), PG.at[tile, 0:ROWS])
                arrive(("ownrow", d), PG.at[tile, ROWS:PACKED])
            else:
                arrive(("y", o, d), PG.at[tile])
            part = PG.at[tile, 0:SPLIT] if d == 0 else PG.at[tile, SPLIT:PACKED]
            send(("relay", o, d), part, part, right if d == 0 else left, s)

    relay(0)
    forward(1)
    forward(3)
    relay(1)
    forward(2)
    relay(3)
    relay(2)

    for c in range(3):
        for e in range(LOCAL):
            for t in (0, COLS + 1):
                X[c, e, t, :, :] = jnp.full((TALL, LANES), float(c != 1), F32)
    for d in (0, 1):
        arrive(("frow", d), FR_in.at[d])
    for c in range(3):
        outside = float(c != 1)
        for e in range(LOCAL):
            row_above = jnp.where(first, outside, FR_in[0, c * LOCAL + e])
            row_below = jnp.where(last, outside, FR_in[1, c * LOCAL + e])
            for t in range(COLS):
                X[c, e, t + 1, HALO - 1 : HALO, :] = row_above[t : t + 1]
                X[c, e, t + 1, HALO + ROWS : HALO + ROWS + 1, :] = row_below[t : t + 1]
    for c in range(2):
        for t in (0, COLS + 1):
            U[c, t, :, :] = jnp.zeros((TALL, LANES), F32)
    for copy in load_n:
        copy.wait()

    for o in range(4):
        tile = ring_tile(o, 2)
        arrive(("relay", o, 0), PG.at[tile, 0:SPLIT])
        arrive(("relay", o, 1), PG.at[tile, SPLIT:PACKED])

    low_tile = lax.broadcasted_iota(jnp.int32, (PACKED, LANES), 1) < TILE

    def unpack(t, speed):
        even, odd = PG[2 * t], PG[2 * t + 1]
        u = jnp.where(low_tile, even, pltpu.roll(odd, TILE, axis=1))
        w = jnp.where(low_tile, pltpu.roll(even, TILE, axis=1), odd)
        for c, strip in ((0, u), (1, w)):
            U[c, t + 1, HALO : HALO + ROWS, :] = strip[0:ROWS]
            U[c, t + 1, HALO - 1 : HALO, :] = strip[ROWS : ROWS + 1]
            U[c, t + 1, HALO + ROWS : HALO + ROWS + 1, :] = strip[ROWS + 1 : ROWS + 2]
        return jnp.maximum(speed, jnp.maximum(even[ROWS + 2 : ROWS + 3], odd[ROWS + 2 : ROWS + 3]))

    speed = lax.fori_loop(0, COLS, unpack, jnp.zeros((1, LANES), F32))
    speed = jnp.max(speed, axis=1, keepdims=True)
    step = COURANT / (speed + SPEED_EPS)
    step = jnp.broadcast_to(step, (8, LANES))
    scale = jnp.sqrt(step / RELAX)

    at_first, at_last = lane == 0, lane == LANES - 1

    def beside(ref, lead, t, rows):
        here = ref[(*lead, t, rows, slice(None))]
        before = ref[(*lead, t - 1, rows, slice(None))]
        after = ref[(*lead, t + 1, rows, slice(None))]
        to_left = pltpu.roll(jnp.where(at_last, before, here), 1, axis=1)
        to_right = pltpu.roll(jnp.where(at_first, after, here), LANES - 1, axis=1)
        return here, to_left, to_right

    def advance(t, tt, row):
        rows = pl.ds(pl.multiple_of(row + HALO, 8), 8)
        rows_above = pl.ds(row + HALO - 1, 8)
        rows_below = pl.ds(row + HALO + 1, 8)
        strip = pl.ds(pl.multiple_of(row, 8), 8)
        u, u_left, u_right = beside(U, (0,), t, rows)
        w, w_left, w_right = beside(U, (1,), t, rows)
        half_step = 0.5 * step
        down_down = half_step * (U[0, t, rows_below, :] - U[0, t, rows_above, :])
        down_across = half_step * (u_right - u_left)
        across_down = half_step * (U[1, t, rows_below, :] - U[1, t, rows_above, :])
        across_across = half_step * (w_right - w_left)
        from_above = step * jnp.maximum(u, 0.0)
        from_below = -step * jnp.minimum(u, 0.0)
        from_left = step * jnp.maximum(w, 0.0)
        from_right = -step * jnp.minimum(w, 0.0)
        relaxed = step / RELAX
        kept = 1.0 - relaxed - (from_above + from_below) - (from_left + from_right)
        own_of = (
            kept + 2.0 * down_down,
            kept + (down_down + across_across),
            kept + 2.0 * across_across,
        )
        twice_across, twice_down = 2.0 * down_across, 2.0 * across_down
        total = [None, None, None]
        for e in range(LOCAL):
            here, new = [], []
            for c in range(3):
                x, x_left, x_right = beside(X, (c, e), t, rows)
                here.append(x)
                value = own_of[c] * x + scale * N[c, e, t - 1, strip, :]
                value += from_above * X[c, e, t, rows_above, :]
                value += from_below * X[c, e, t, rows_below, :]
                value += from_left * x_left + from_right * x_right
                new.append(value)
            new[0] += twice_across * here[1] + relaxed
            new[1] += down_across * here[2] + across_down * here[0]
            new[2] += twice_down * here[1] + relaxed
            for c in range(3):
                N[c, e, t - 1, strip, :] = new[c]
                total[c] = new[c] if e == 0 else total[c] + new[c]
        columns = pl.ds(pl.multiple_of((t - 1) * LANES, LANES), LANES)
        weight = MODULUS / FIELDS * G[strip, columns].astype(F32)
        return (
            weight * (total[0] - float(LOCAL)),
            weight * total[1],
            weight * (total[2] - float(LOCAL)),
        )

    def evolve(j):
        block = (zh + ORDER[j]) % RING

        def body(i, carry):
            tt, r = i // 4, i % 4
            t = 2 * block + tt + 1
            folded = []
            for part in (0, 1):
                row = (r + 4 * part) * 8
                xx, xy, yy = advance(t, tt, row)
                strip = pl.ds(pl.multiple_of(row, 8), 8)
                Q[j, 2 * tt, strip, :] = jnp.where(low, xx, pltpu.roll(xy, TILE, axis=1))
                Q[j, 2 * tt + 1, strip, :] = jnp.where(low, pltpu.roll(xx, TILE, axis=1), xy)
                folded.append(yy)
            strip = pl.ds(pl.multiple_of(r * 8 + ROWS, 8), 8)
            top, bottom = folded
            Q[j, 2 * tt, strip, :] = jnp.where(low, top, pltpu.roll(bottom, TILE, axis=1))
            Q[j, 2 * tt + 1, strip, :] = jnp.where(low, pltpu.roll(top, TILE, axis=1), bottom)
            return carry

        lax.fori_loop(0, 8, body, 0)
        stores = []
        for tt in (0, 1):
            t = 2 * block + tt
            columns = pl.ds(pl.multiple_of(t * LANES, LANES), LANES)
            store = pltpu.make_async_copy(
                N.at[:, :, t], fields_out.at[:, :, :, columns], out_sem.at[2 * j + tt]
            )
            store.start()
            stores.append(store)
        return stores

    y_up, y_down, y_far = (y + 1) % RING, (y + 3) % RING, (y + 2) % RING

    def ring_far(j):
        send(("half", j, 0), Q.at[j, y_far, 0:HALF], H_in.at[j, 0:HALF], right, s)
        send(("half", j, 1), Q.at[j, y_far, HALF:STRESS], H_in.at[j, HALF:STRESS], left, s)

    def ring_near(j):
        arrive(("half", j, 0), H_in.at[j, 0:HALF])
        Q[j, y_up, 0:HALF, :] += H_in[j, 0:HALF, :]
        send(("whole", j, 0), Q.at[j, y_up], W_in.at[j, 0], right, s)
        arrive(("half", j, 1), H_in.at[j, HALF:STRESS])
        Q[j, y_down, HALF:STRESS, :] += H_in[j, HALF:STRESS, :]
        send(("whole", j, 1), Q.at[j, y_down], W_in.at[j, 1], left, s)

    def ring_sum(j):
        arrive(("whole", j, 0), W_in.at[j, 0])
        arrive(("whole", j, 1), W_in.at[j, 1])
        T[j] = Q[j, y] + (W_in[j, 0] + W_in[j, 1])
        if ORDER[j]:
            send(("reduced", j), T.at[j], Z_in.at[j], z_peer(ORDER[j]), s)

    stores = []
    for j in range(4):
        stores += evolve(j)
        ring_far(j)
        if j >= 1:
            ring_near(j - 1)
        if j >= 2:
            ring_sum(j - 2)
    ring_near(3)
    ring_sum(2)

    at_row = lax.broadcasted_iota(jnp.int32, (TALL, LANES), 0) + (s * ROWS - HALO)
    at_lane = lax.broadcasted_iota(jnp.int32, (TALL, LANES), 1)
    at_col = at_lane + (f * TILE - HALO)
    inside = (at_row >= 0) & (at_row < TILES * ROWS) & (at_col >= 0) & (at_col < TILES * TILE)
    inside = inside & (at_lane < TALL)
    for d in (0, 1):
        arrive(("vcorner", d), VC_in.at[d])

    def stacked(rim_rows, tile):
        return jnp.concatenate([rim_rows[0:8], PG[tile, 0:ROWS, :], rim_rows[8:16]], axis=0)

    v_mid = stacked(VC_out, f)
    v_left = stacked(VC_in.at[0], f_down)
    v_right = stacked(VC_in.at[1], f_up)

    def window(before, here, after):
        return jnp.where(at_lane < HALO, before, jnp.where(at_lane < HALO + TILE, here, after))

    near = lambda v: pltpu.roll(v, HALO, axis=1)
    far = lambda v: pltpu.roll(v, HALO + TILE, axis=1)
    speeds = (
        jnp.where(inside, window(far(v_left), near(v_mid), far(v_right)), 0.0),
        jnp.where(inside, window(near(v_left), far(v_mid), near(v_right)), 0.0),
    )
    mask = jnp.concatenate([VR_in[0, 8:16, :], walls(slice(0, ROWS)), VR_in[1, 8:16, :]], axis=0)
    weight = BETA + 4.0 * VISCOSITY + PENALTY * (1.0 - mask)

    def around(values):
        return (
            pltpu.roll(values, TALL - 1, axis=0)
            + pltpu.roll(values, 1, axis=0)
            + pltpu.roll(values, LANES - 1, axis=1)
            + pltpu.roll(values, 1, axis=1)
        )

    def apply(values):
        return weight * values - VISCOSITY * around(values)

    ring_sum(3)
    total = T[3]
    for j in range(3):
        arrive(("reduced", j), Z_in.at[j])
        total = total + Z_in[j]
    xx_xy, yy = total[0:ROWS], total[ROWS:STRESS]
    tile_stress = (near(xx_xy), far(xx_xy), jnp.concatenate([near(yy), far(yy)], axis=0))
    edges = jnp.zeros((ROWS, LANES), F32)
    at_edge = lax.broadcasted_iota(jnp.int32, (ROWS, LANES), 1)
    for c in range(3):
        E[c, :, :] = tile_stress[c]
        low_edge = pltpu.roll(tile_stress[c], LANES - TILE + 8 * c, axis=1)
        high_edge = pltpu.roll(tile_stress[c], 16 + 8 * c, axis=1)
        edges = jnp.where((at_edge >= 8 * c) & (at_edge < 8 * c + 8), low_edge, edges)
        edges = jnp.where((at_edge >= 24 + 8 * c) & (at_edge < 32 + 8 * c), high_edge, edges)
    B[...] = edges
    for a, to_f in ((0, f_up), (1, f_down)):
        send(("edge", a), B, B_in.at[a, HALO : HALO + ROWS], to_f, s)
    for b, to_s in ((0, s_up), (1, s_down)):
        rows = slice(ROWS - 8, ROWS) if b == 0 else slice(0, 8)
        send(("srow", b), E.at[:, rows], E_in.at[b], f, to_s)
        for a, to_f in ((0, f_up), (1, f_down)):
            landing = slice(0, 8) if b == 0 else slice(HALO + ROWS, TALL)
            send(("corner", a, b), B.at[rows], B_in.at[a, landing], to_f, to_s)

    residual = [BETA * v - apply(v) for v in speeds]

    for b in (0, 1):
        arrive(("srow", b), E_in.at[b])
        for a in (0, 1):
            landing = slice(0, 8) if b == 0 else slice(HALO + ROWS, TALL)
            arrive(("corner", a, b), B_in.at[a, landing])
    for a in (0, 1):
        arrive(("edge", a), B_in.at[a, HALO : HALO + ROWS])
    stress = []
    for c in range(3):
        middle = jnp.concatenate([E_in[0, c], E[c], E_in[1, c]], axis=0)
        before = pltpu.roll(B_in[0], (LANES - 8 * c) % LANES, axis=1)
        after = pltpu.roll(B_in[1], 48 - 8 * c, axis=1)
        stress.append(jnp.where(inside, window(before, middle, after), 0.0))

    def along_rows(values):
        return pltpu.roll(values, TALL - 1, axis=0) - pltpu.roll(values, 1, axis=0)

    def along_cols(values):
        return pltpu.roll(values, LANES - 1, axis=1) - pltpu.roll(values, 1, axis=1)

    force = (
        0.5 * (along_rows(stress[0]) + along_cols(stress[1])),
        0.5 * (along_rows(stress[1]) + along_cols(stress[2])),
    )
    centre = 0.5 * (UPPER + LOWER)
    radius = 0.5 * (UPPER - LOWER)
    sigma = centre / radius
    for c in range(2):
        rho = 1.0 / sigma
        v = speeds[c]
        r = jnp.where(inside, residual[c] + force[c], 0.0)
        d = r / centre
        for index in range(ITERS):
            v = v + d
            if index + 1 < ITERS:
                r = jnp.where(inside, r - apply(d), 0.0)
                rho_next = 1.0 / (2.0 * sigma - rho)
                d = rho_next * rho * d + 2.0 * rho_next / radius * r
                rho = rho_next
        velocity_out[c, :, :] = pltpu.roll(v, LANES - HALO, axis=1)[HALO : HALO + ROWS, 0:TILE]

    for copy in started:
        copy.wait_send()
    for store in stores:
        store.wait()


def per_device(fields, increments, velocity, geometry):
    anywhere = pl.BlockSpec(memory_space=pl.ANY)

    def vmem(*shape):
        return pltpu.VMEM(shape, F32)

    return pl.pallas_call(
        kernel,
        out_shape=(
            jax.ShapeDtypeStruct(fields.shape, F32),
            jax.ShapeDtypeStruct(velocity.shape, F32),
        ),
        in_specs=[anywhere] * 4,
        out_specs=(anywhere, pl.BlockSpec(memory_space=pltpu.VMEM)),
        scratch_shapes=[
            vmem(3, LOCAL, COLS + 2, TALL, LANES),
            vmem(3, LOCAL, COLS, ROWS, LANES),
            vmem(2, ROWS, TILE),
            pltpu.VMEM((ROWS, COLS * LANES), jnp.int32),
            vmem(2, COLS + 2, TALL, LANES),
            vmem(TILES, PACKED, LANES),
            vmem(8, LANES),
            vmem(TILES, 8, LANES),
            vmem(2, 16, LANES),
            vmem(2, 16, LANES),
            vmem(2, 3 * LOCAL, COLS, LANES),
            vmem(2, 3 * LOCAL, COLS, LANES),
            vmem(16, LANES),
            vmem(2, 16, LANES),
            vmem(RING, RING, STRESS, LANES),
            vmem(RING, STRESS, LANES),
            vmem(RING, 2, STRESS, LANES),
            vmem(3, STRESS, LANES),
            vmem(RING, STRESS, LANES),
            vmem(3, ROWS, LANES),
            vmem(ROWS, LANES),
            vmem(2, TALL, LANES),
            vmem(2, 3, 8, LANES),
            pltpu.SemaphoreType.DMA((2 + 2 * COLS,)),
            pltpu.SemaphoreType.DMA((COLS,)),
            pltpu.SemaphoreType.DMA((len(SLOTS),)),
            pltpu.SemaphoreType.DMA((len(SLOTS),)),
        ],
        compiler_params=pltpu.CompilerParams(
            collective_id=0, has_side_effects=True, vmem_limit_bytes=40 * 1024 * 1024
        ),
        name="step",
    )(fields, increments, velocity, geometry)


def solution(mesh):
    placed = (
        P(None, "field", "space", None),
        P(None, "field", "space", None),
        P(None, "space", "field"),
        P("space", None),
    )
    return jax.shard_map(
        per_device,
        mesh=mesh,
        in_specs=placed,
        out_specs=(P(None, "field", "space", None), P(None, "space", "field")),
        check_vma=False,
    )
```

time: 492 us -> 67.6 us (0.14)
  the two profiles are of different devices: /device:TPU:120 before, /device:TPU:1 now
where the time goes in v1:
time: 67.6 us; the launch traced here: 67.3 us
  Pallas kernels  58.8 us (87%)
  local copies, waits for them, and re-layouts  7.86 us (12%)
    pallas_call x1, Pallas kernels, per_device(): pl.pallas_call(kernel, out_shape=(jax.ShapeDtypeStruct(fields.shape, F32)...  58.8 us
    unnamed x10, local copies, waits for them, and re-layouts  7.86 us

profile of v1, /device:TPU:1, one launch (start us, length us, event | category | flops | bytes accessed | tf_op | source)
XLA Modules:
  0.0 67.3 jit_solution(12317612895763239495)
XLA Ops:
  0.6 0.0 copy-start
  0.6 1.9 %copy-done = f32[3,4,64,1024]{3,2,1,0:T(8,128)S(1)} copy-done((f32[3,4,64,1024]{3,2,1,0:T(8,128)S(1)}, f32[3,4,64,1024]{3,2,1,0:T(8,128)}, u32[]{:S(2)}) %copy-start) | copy-done | bytes 3145752
  2.5 0.0 copy-start.1
  2.5 1.9 %copy-done.1 = f32[3,4,64,1024]{3,2,1,0:T(8,128)S(1)} copy-done((f32[3,4,64,1024]{3,2,1,0:T(8,128)S(1)}, f32[3,4,64,1024]{3,2,1,0:T(8,128)}, u32[]{:S(2)}) %copy-start.1) | copy-done | bytes 3145752
  4.4 0.0 copy-start.2
  4.4 0.9 %copy-done.2 = s32[64,1024]{1,0:T(8,128)S(1)} copy-done((s32[64,1024]{1,0:T(8,128)S(1)}, s32[64,1024]{1,0:T(8,128)}, u32[]{:S(2)}) %copy-start.2) | copy-done | bytes 262168
  5.4 0.0 copy-start.3
  5.4 0.8 %copy-done.3 = f32[2,64,64]{2,1,0:T(8,128)S(1)} copy-done((f32[2,64,64]{2,1,0:T(8,128)S(1)}, f32[2,64,64]{2,1,0:T(8,128)}, u32[]{:S(2)}) %copy-start.3) | copy-done | bytes 32792
  6.2 58.8 %step.1 = (f32[3,4,64,1024]{3,2,1,0:T(8,128)S(1)}, f32[2,64,64]{2,1,0:T(8,128)S(1)}) custom-call(f32[3,4,64,1024]{3,2,1,0:T(8,128)S(1)} %copy-done, f32[3,4,64,1024]{3,2,1,0:T(8,128)S(1)} %copy-done.1, f32[2,64,64]{2,1,0:T(8,128)S(1)} %copy-done.3, s32[64,1024]{1,0:T(8,128)S(1)} %copy-done.2), custom_call_target="tpu_custom_call" | custom-call | tf_op jit(solution)/shard_map/step/pallas_call | solution.py:513
  65.0 1.7 %copy.8 = f32[3,4,64,1024]{3,2,1,0:T(8,128)} copy(f32[3,4,64,1024]{3,2,1,0:T(8,128)S(1)} %get-tuple-element.4) | data formatting | bytes 6291456
  66.7 0.6 copy.9
Async XLA Ops:
  0.6 1.9 %copy-start = (f32[3,4,64,1024]{3,2,1,0:T(8,128)S(1)}, f32[3,4,64,1024]{3,2,1,0:T(8,128)}, u32[]{:S(2)}) copy-start(f32[3,4,64,1024]{3,2,1,0:T(8,128)} %fields.1) | copy-start | bytes 9437188
  2.5 1.9 %copy-start.1 = (f32[3,4,64,1024]{3,2,1,0:T(8,128)S(1)}, f32[3,4,64,1024]{3,2,1,0:T(8,128)}, u32[]{:S(2)}) copy-start(f32[3,4,64,1024]{3,2,1,0:T(8,128)} %noise.1) | copy-start | bytes 9437188
  4.4 0.9 %copy-start.2 = (s32[64,1024]{1,0:T(8,128)S(1)}, s32[64,1024]{1,0:T(8,128)}, u32[]{:S(2)}) copy-start(s32[64,1024]{1,0:T(8,128)} %geometry.1) | copy-start | bytes 786436
  5.4 0.8 %copy-start.3 = (f32[2,64,64]{2,1,0:T(8,128)S(1)}, f32[2,64,64]{2,1,0:T(8,128)}, u32[]{:S(2)}) copy-start(f32[2,64,64]{2,1,0:T(8,128)} %velocity.1) | copy-start | bytes 98308

commit v2 on v1

v2 whole, which is shorter than its diff:
```python
import functools

import jax
import jax.numpy as jnp
from jax import lax
from jax.experimental import pallas as pl
from jax.experimental.pallas import tpu as pltpu
from jax.sharding import PartitionSpec as P

ITERS = 8
COURANT = 0.5
SPEED_EPS = 1e-06
RELAX = 0.5
MODULUS = 2.0
BETA = 0.5
VISCOSITY = 1.0
PENALTY = 20.0
LOWER = BETA
UPPER = BETA + PENALTY + 8.0 * VISCOSITY

MESH = pl.DeviceIdType.MESH
F32 = jnp.float32
LANES = 128
ROWS = 64
HALO = 8
TALL = ROWS + 2 * HALO
TILE = 64
TILES = 16
COLS = 8
FIELDS = 64
LOCAL = 4
VMEM_LIMIT = 63 * 1024 * 1024
RING = 4
PACKED = 72
EDGE = 12 * 3 + 1


def slots():
    names = [(n, d) for n in ("max", "rim") for d in range(1, 16)]
    names += [(n, d) for n in ("vrow", "frow", "vcorner", "side", "end") for d in (0, 1)]
    names += [(n, d) for n in ("z", "y") for d in (1, 2, 3)]
    names += [("zy", o, d) for o in (1, 2, 3) for d in (1, 2, 3)]
    names += [("part", j, d) for j in range(4) for d in (1, 2, 3)]
    names += [("sum", j) for j in range(3)]
    names += [("corner", a, b) for a in (0, 1) for b in (0, 1)]
    return {name: at for at, name in enumerate(names)}


SLOTS = slots()


def coefficients(step, u, w):
    (u, u_above, u_below, u_left, u_right), (w, w_above, w_below, w_left, w_right) = u, w
    half_step = 0.5 * step
    down_down = half_step * (u_below - u_above)
    down_across = half_step * (u_right - u_left)
    across_down = half_step * (w_below - w_above)
    across_across = half_step * (w_right - w_left)
    from_above = step * jnp.maximum(u, 0.0)
    from_below = -step * jnp.minimum(u, 0.0)
    from_left = step * jnp.maximum(w, 0.0)
    from_right = -step * jnp.minimum(w, 0.0)
    relaxed = step / RELAX
    kept = 1.0 - relaxed - (from_above + from_below) - (from_left + from_right)
    own = (
        kept + 2.0 * down_down,
        kept + (down_down + across_across),
        kept + 2.0 * across_across,
    )
    return own, (from_above, from_below, from_left, from_right), down_across, across_down, relaxed


def update(weights, scale, tensors, noises):
    own, sides, down_across, across_down, relaxed = weights
    new = []
    for c in range(3):
        value = own[c] * tensors[c][0] + scale * noises[c]
        for side, beside in zip(sides, tensors[c][1:]):
            value = value + side * beside
        new.append(value)
    xx, xy, yy = (tensor[0] for tensor in tensors)
    return (
        new[0] + (2.0 * down_across * xy + relaxed),
        new[1] + (down_across * yy + across_down * xx),
        new[2] + (2.0 * across_down * xy + relaxed),
    )


def kernel(
    fields, noise, velocity, geometry, fields_out, velocity_out,
    X, N, V, G, U, UE, S, PG, M_own, M_all, VR_out, VR_in, FE_out, FE_in, VC_out, VC_in,
    Q, Y_in, Z_in, T, F, F_in, E_in, local_sem, send_sem, recv_sem,
):
    f = lax.axis_index("field")
    s = lax.axis_index("space")
    zh = f // RING
    y = f % RING
    f_up, f_down = (f + 1) % TILES, (f + TILES - 1) % TILES
    s_up, s_down = (s + 1) % TILES, (s + TILES - 1) % TILES
    first, last = s == 0, s == TILES - 1

    def y_peer(d):
        return zh * RING + (y + d) % RING

    def z_peer(o):
        return (zh + o) % RING * RING + y

    def peer_back(o, d):
        return (zh + RING - o) % RING * RING + (y + RING - d) % RING

    started = []

    def send(name, source, target, to_f, to_s):
        copy = pltpu.make_async_remote_copy(
            src_ref=source,
            dst_ref=target,
            send_sem=send_sem.at[SLOTS[name]],
            recv_sem=recv_sem.at[SLOTS[name]],
            device_id=(to_f, to_s),
            device_id_type=MESH,
        )
        copy.start()
        started.append(copy)

    def arrive(name, landed):
        pltpu.make_async_copy(landed, landed, recv_sem.at[SLOTS[name]]).wait()

    barrier = pltpu.get_barrier_semaphore()
    partners = [(f, (s + d) % TILES) for d in range(1, TILES)]
    partners += [((f + d) % TILES, s) for d in range(1, TILES)]
    partners += [(a, b) for a in (f_up, f_down) for b in (s_up, s_down)]
    for partner in partners:
        pl.semaphore_signal(barrier, inc=1, device_id=partner, device_id_type=MESH)

    load_v = pltpu.make_async_copy(velocity, V, local_sem.at[0])
    load_v.start()
    load_g = pltpu.make_async_copy(geometry, G, local_sem.at[1])
    load_g.start()
    loads = []
    for c in range(3):
        inner = X.at[c, :, HALO : HALO + ROWS, LANES : LANES + COLS * LANES]
        loads.append(pltpu.make_async_copy(fields.at[c], inner, local_sem.at[2 + c]))
    for c in range(3):
        loads.append(pltpu.make_async_copy(noise.at[c], N.at[c], local_sem.at[5 + c]))
    for copy in loads:
        copy.start()

    lane = lax.broadcasted_iota(jnp.int32, (8, LANES), 1)
    row = lax.broadcasted_iota(jnp.int32, (8, LANES), 0)
    low = lane < TILE
    at_left, at_right = lane == 0, lane == LANES - 1
    at_top, at_bottom = row == 0, row == 7

    load_v.wait()
    own = jnp.concatenate([V[0], V[1]], axis=1)
    PG[f, 0:ROWS, :] = own
    M_own[...] = jnp.max(jnp.abs(own).reshape(ROWS // 8, 8, LANES), axis=0)
    VR_out[0, 0:8, :] = own[ROWS - 8 :]
    VR_out[1, 0:8, :] = own[0:8]

    load_g.wait()
    half = f % 2
    t_own = f // 2

    def walls(rows):
        def block(t):
            at = pl.multiple_of(jnp.clip(t, 0, COLS - 1) * LANES, LANES)
            return G[rows, pl.ds(at, LANES)].astype(F32)

        before, here, after = block(t_own - 1), block(t_own), block(t_own + 1)
        count = here.shape[0]
        at = lax.broadcasted_iota(jnp.int32, (count, LANES), 1)
        even = pltpu.roll(jnp.where(at < 120, here, before), HALO, axis=1)
        odd = pltpu.roll(jnp.where(at < HALO, after, here), HALO + TILE, axis=1)
        return jnp.where(half == 0, even, odd)

    VR_out[0, 8:16, :] = walls(slice(ROWS - 8, ROWS))
    VR_out[1, 8:16, :] = walls(slice(0, 8))

    pl.semaphore_wait(barrier, len(partners))

    main = PG.at[f, 0:ROWS]
    for o in (2, 1, 3):
        send(("z", o), main, main, z_peer(o), s)
    for d in (2, 1, 3):
        send(("y", d), main, main, y_peer(d), s)
    send(("vrow", 0), VR_out.at[0], VR_in.at[0], f, s_up)
    send(("vrow", 1), VR_out.at[1], VR_in.at[1], f, s_down)
    for d in range(1, TILES):
        send(("max", d), M_own, M_all.at[d], f, (s + d) % TILES)

    for copy in loads:
        copy.wait()
    for t in range(COLS):
        columns = slice(t * LANES, (t + 1) * LANES)
        inner = slice((t + 1) * LANES, (t + 2) * LANES)
        here = slice(t, t + 1)
        for c in range(3):
            for e in range(LOCAL):
                at = c * LOCAL + e
                for side, edge, step in ((0, ROWS - 1, -1), (1, 0, 1)):
                    near = HALO + edge
                    FE_out[side, at, here, :] = X[c, e, near : near + 1, inner]
                    FE_out[side, 12 + at, here, :] = X[c, e, near + step : near + step + 1, inner]
                    FE_out[side, 24 + at, here, :] = N[c, e, edge : edge + 1, columns]
        for side, edge in ((0, ROWS - 1), (1, 0)):
            FE_out[side, EDGE - 1, here, :] = G[edge : edge + 1, columns].astype(F32)
    send(("frow", 0), FE_out.at[0], FE_in.at[0], f, s_up)
    send(("frow", 1), FE_out.at[1], FE_in.at[1], f, s_down)

    for d in (0, 1):
        arrive(("vrow", d), VR_in.at[d])
    speed = M_own[...]
    for d in range(1, TILES):
        arrive(("max", d), M_all.at[d])
        speed = jnp.maximum(speed, M_all[d])
    speed = jnp.max(speed, axis=0, keepdims=True)
    above = jnp.where(first, 0.0, VR_in[0, 6:8, :])
    below = jnp.where(last, 0.0, VR_in[1, 0:2, :])
    PG[f, ROWS : ROWS + 2, :] = above
    PG[f, ROWS + 2 : ROWS + 4, :] = below
    PG[f, ROWS + 4 : PACKED, :] = jnp.broadcast_to(speed, (PACKED - ROWS - 4, LANES))
    rim = PG.at[f, ROWS:PACKED]
    for d in range(1, TILES):
        send(("rim", d), rim, rim, (f + d) % TILES, s)

    for o in (1, 3, 2):
        tile = PG.at[peer_back(o, 0), 0:ROWS]
        arrive(("z", o), tile)
        for d in (2, 1, 3):
            send(("zy", o, d), tile, tile, y_peer(d), s)
    VC_out[0:8, :] = VR_in[0, 0:8, :]
    VC_out[8:16, :] = VR_in[1, 0:8, :]
    send(("vcorner", 0), VC_out, VC_in.at[0], f_up, s)
    send(("vcorner", 1), VC_out, VC_in.at[1], f_down, s)

    for c in range(3):
        for e in range(LOCAL):
            for t in (0, COLS + 1):
                outer = slice(t * LANES, (t + 1) * LANES)
                X[c, e, :, outer] = jnp.full((TALL, LANES), float(c != 1), F32)
    for t in (0, COLS + 1):
        U[:, :, t * LANES : (t + 1) * LANES] = jnp.zeros((2, TALL, LANES), F32)
        S[:, t, :, :] = jnp.zeros((3, TALL, LANES), F32)
    for d in (0, 1):
        arrive(("frow", d), FE_in.at[d])
    for c in range(3):
        outside = float(c != 1)
        for e in range(LOCAL):
            row_above = jnp.where(first, outside, FE_in[0, c * LOCAL + e])
            row_below = jnp.where(last, outside, FE_in[1, c * LOCAL + e])
            for t in range(COLS):
                inner = slice((t + 1) * LANES, (t + 2) * LANES)
                X[c, e, HALO - 1 : HALO, inner] = row_above[t : t + 1]
                X[c, e, HALO + ROWS : HALO + ROWS + 1, inner] = row_below[t : t + 1]

    for d in (1, 2, 3):
        arrive(("y", d), PG.at[peer_back(0, d), 0:ROWS])
    for o in (1, 3, 2):
        for d in (1, 2, 3):
            arrive(("zy", o, d), PG.at[peer_back(o, d), 0:ROWS])
    for d in range(1, TILES):
        arrive(("rim", d), PG.at[(f + TILES - d) % TILES, ROWS:PACKED])

    low_tile = lax.broadcasted_iota(jnp.int32, (PACKED, LANES), 1) < TILE
    speed = jnp.zeros((1, LANES), F32)
    for t in range(COLS):
        even, odd = PG[2 * t], PG[2 * t + 1]
        u = jnp.where(low_tile, even, pltpu.roll(odd, TILE, axis=1))
        w = jnp.where(low_tile, pltpu.roll(even, TILE, axis=1), odd)
        columns = slice((t + 1) * LANES, (t + 2) * LANES)
        here = slice(t, t + 1)
        for c, strip in ((0, u), (1, w)):
            U[c, HALO : HALO + ROWS, columns] = strip[0:ROWS]
            U[c, HALO - 2 : HALO, columns] = strip[ROWS : ROWS + 2]
            U[c, HALO + ROWS : HALO + ROWS + 2, columns] = strip[ROWS + 2 : ROWS + 4]
            UE[0, c, 0, here, :] = strip[ROWS + 1 : ROWS + 2]
            UE[0, c, 1, here, :] = strip[ROWS : ROWS + 1]
            UE[0, c, 2, here, :] = strip[0:1]
            UE[1, c, 0, here, :] = strip[ROWS + 2 : ROWS + 3]
            UE[1, c, 1, here, :] = strip[ROWS - 1 : ROWS]
            UE[1, c, 2, here, :] = strip[ROWS + 3 : ROWS + 4]
        speed = jnp.maximum(speed, jnp.maximum(even[ROWS + 4 : ROWS + 5], odd[ROWS + 4 : ROWS + 5]))
    speed = jnp.max(speed, axis=1, keepdims=True)
    step = COURANT / (speed + SPEED_EPS)
    step = jnp.broadcast_to(step, (8, LANES))
    scale = jnp.sqrt(step / RELAX)

    def stress_of(total, weight):
        weight = MODULUS / FIELDS * weight
        return (
            weight * (total[0] - float(LOCAL)),
            weight * total[1],
            weight * (total[2] - float(LOCAL)),
        )

    def added(total, new):
        return new if total is None else tuple(a + b for a, b in zip(total, new))

    def spread(centre, above, below, outside):
        to_right = pltpu.roll(centre, 1, axis=1)
        to_left = pltpu.roll(centre, LANES - 1, axis=1)
        before = jnp.where(at_top, outside, pltpu.roll(to_right, 1, axis=0))
        after = jnp.where(at_bottom, outside, pltpu.roll(to_left, 7, axis=0))
        left = jnp.where(at_left, before, to_right)
        right = jnp.where(at_right, after, to_left)
        return centre, above, below, left, right

    for side, absent, place in ((0, first, HALO - 1), (1, last, HALO + ROWS)):
        weights = coefficients(step, *(spread(*(UE[side, c, q] for q in range(3)), 0.0) for c in range(2)))
        total = None
        for e in range(LOCAL):
            tensors = []
            for c in range(3):
                at = c * LOCAL + e
                centre, outer, inner = FE_in[side, at], FE_in[side, 12 + at], FE_out[1 - side, at]
                above, below = (outer, inner) if side == 0 else (inner, outer)
                tensors.append(spread(centre, above, below, float(c != 1)))
            noises = [FE_in[side, 24 + c * LOCAL + e] for c in range(3)]
            total = added(total, update(weights, scale, tensors, noises))
        for c, values in enumerate(stress_of(total, FE_in[side, EDGE - 1])):
            values = jnp.where(absent, 0.0, values)
            for t in range(COLS):
                S[c, t + 1, place : place + 1, :] = values[t : t + 1]

    def block_at(t):
        return pl.ds(pl.multiple_of(t * LANES, LANES), LANES)

    def nearby(ref, lead, r, t):
        rows, columns = pl.ds(pl.multiple_of(r * 8 + HALO, 8), 8), block_at(t)
        rows_above = pl.ds(pl.multiple_of(r * 8, 8), 8)
        rows_below = pl.ds(pl.multiple_of(r * 8 + 2 * HALO, 8), 8)
        here = ref[(*lead, rows, columns)]
        above = jnp.where(at_bottom, ref[(*lead, rows_above, columns)], here)
        below = jnp.where(at_top, ref[(*lead, rows_below, columns)], here)
        left = jnp.where(at_right, ref[(*lead, rows, block_at(t - 1))], here)
        right = jnp.where(at_left, ref[(*lead, rows, block_at(t + 1))], here)
        return (
            here,
            pltpu.roll(above, 1, axis=0),
            pltpu.roll(below, 7, axis=0),
            pltpu.roll(left, 1, axis=1),
            pltpu.roll(right, LANES - 1, axis=1),
        )

    start = 2 * ((zh + 1) % RING) + COLS - 1

    def advance(i, carry):
        t = (start + i // 8) % COLS + 1
        r = i % 8
        rows, columns = pl.ds(pl.multiple_of(r * 8, 8), 8), block_at(t - 1)
        weights = coefficients(step, nearby(U, (0,), r, t), nearby(U, (1,), r, t))
        total = None
        for e in range(LOCAL):
            tensors = [nearby(X, (c, e), r, t) for c in range(3)]
            noises = [N[c, e, rows, columns] for c in range(3)]
            new = update(weights, scale, tensors, noises)
            for c in range(3):
                N[c, e, rows, columns] = new[c]
            total = added(total, new)
        weight = G[rows, columns].astype(F32)
        for c, values in enumerate(stress_of(total, weight)):
            S[c, t, pl.ds(pl.multiple_of(r * 8 + HALO, 8), 8), :] = values
        return carry

    def forces(j):
        block = (zh + 1 + j) % RING

        def body(i, carry):
            tt, r = i // 8, i % 8
            t = 2 * block + tt + 1
            rows = pl.ds(pl.multiple_of(r * 8 + HALO, 8), 8)

            def along_rows(c):
                return S[c, t, pl.ds(r * 8 + HALO + 1, 8), :] - S[c, t, pl.ds(r * 8 + HALO - 1, 8), :]

            def along_cols(c):
                here = S[c, t, rows, :]
                left = jnp.where(at_right, S[c, t - 1, rows, :], here)
                right = jnp.where(at_left, S[c, t + 1, rows, :], here)
                return pltpu.roll(right, LANES - 1, axis=1) - pltpu.roll(left, 1, axis=1)

            down = 0.5 * (along_rows(0) + along_cols(1))
            across = 0.5 * (along_rows(1) + along_cols(2))
            rows = pl.ds(pl.multiple_of(r * 8, 8), 8)
            Q[j, 2 * tt, rows, :] = jnp.where(low, down, pltpu.roll(across, TILE, axis=1))
            Q[j, 2 * tt + 1, rows, :] = jnp.where(low, pltpu.roll(down, TILE, axis=1), across)
            return carry

        lax.fori_loop(0, 16, body, 0)
        for d in (2, 1, 3):
            send(("part", j, d), Q.at[j, (y + d) % RING], Y_in.at[j, d - 1], y_peer(d), s)

    def ring_sum(j):
        for d in (1, 2, 3):
            arrive(("part", j, d), Y_in.at[j, d - 1])
        T[j] = (Q[j, y] + Y_in[j, 0]) + (Y_in[j, 1] + Y_in[j, 2])
        if j < 3:
            send(("sum", j), T.at[j], Z_in.at[j], z_peer(j + 1), s)

    lax.fori_loop(0, 32, advance, 0)
    forces(0)
    lax.fori_loop(32, 48, advance, 0)
    forces(1)
    lax.fori_loop(48, 64, advance, 0)
    forces(2)
    forces(3)
    store = pltpu.make_async_copy(N, fields_out, local_sem.at[8])
    store.start()
    ring_sum(0)
    ring_sum(1)
    ring_sum(2)

    at_row = lax.broadcasted_iota(jnp.int32, (TALL, LANES), 0) + (s * ROWS - HALO)
    at_lane = lax.broadcasted_iota(jnp.int32, (TALL, LANES), 1)
    at_col = at_lane + (f * TILE - HALO)
    inside = (at_row >= 0) & (at_row < TILES * ROWS) & (at_col >= 0) & (at_col < TILES * TILE)
    inside = inside & (at_lane < TALL)
    for d in (0, 1):
        arrive(("vcorner", d), VC_in.at[d])

    def windows(before, here, after):
        near = lambda v: pltpu.roll(v, HALO, axis=1)
        far = lambda v: pltpu.roll(v, HALO + TILE, axis=1)

        def window(a, b, c):
            joined = jnp.where(at_lane < HALO, a, jnp.where(at_lane < HALO + TILE, b, c))
            return jnp.where(inside, joined, 0.0)

        return (
            window(far(before), near(here), far(after)),
            window(near(before), far(here), near(after)),
        )

    def stacked(rim_rows, tile):
        return jnp.concatenate([rim_rows[0:8], PG[tile, 0:ROWS, :], rim_rows[8:16]], axis=0)

    speeds = windows(
        stacked(VC_in.at[0], f_down), stacked(VC_out, f), stacked(VC_in.at[1], f_up)
    )
    mask = jnp.concatenate([VR_in[0, 8:16, :], walls(slice(0, ROWS)), VR_in[1, 8:16, :]], axis=0)
    weight = BETA + 4.0 * VISCOSITY + PENALTY * (1.0 - mask)

    def apply(values):
        around = (
            pltpu.roll(values, TALL - 1, axis=0)
            + pltpu.roll(values, 1, axis=0)
            + pltpu.roll(values, LANES - 1, axis=1)
            + pltpu.roll(values, 1, axis=1)
        )
        return weight * values - VISCOSITY * around

    residual = [BETA * v - apply(v) for v in speeds]

    ring_sum(3)
    total = T[3]
    for j in range(3):
        arrive(("sum", j), Z_in.at[j])
        total = total + Z_in[j]
    F[...] = total
    for b, to_s in ((0, s_up), (1, s_down)):
        rows = slice(ROWS - 8, ROWS) if b == 0 else slice(0, 8)
        landing = slice(0, 8) if b == 0 else slice(HALO + ROWS, TALL)
        for a, to_f in ((0, f_up), (1, f_down)):
            send(("corner", a, b), F.at[rows], F_in.at[a, landing], to_f, to_s)
    for a, to_f in ((0, f_up), (1, f_down)):
        send(("side", a), F, F_in.at[a, HALO : HALO + ROWS], to_f, s)
    for b, to_s in ((0, s_up), (1, s_down)):
        rows = slice(ROWS - 8, ROWS) if b == 0 else slice(0, 8)
        send(("end", b), F.at[rows], E_in.at[b], f, to_s)
    for b in (0, 1):
        arrive(("end", b), E_in.at[b])
    for a in (0, 1):
        arrive(("side", a), F_in.at[a, HALO : HALO + ROWS])
    for b in (0, 1):
        for a in (0, 1):
            landing = slice(0, 8) if b == 0 else slice(HALO + ROWS, TALL)
            arrive(("corner", a, b), F_in.at[a, landing])
    force = windows(F_in[0], jnp.concatenate([E_in[0], F[...], E_in[1]], axis=0), F_in[1])

    centre = 0.5 * (UPPER + LOWER)
    radius = 0.5 * (UPPER - LOWER)
    sigma = centre / radius
    for c in range(2):
        rho = 1.0 / sigma
        v = speeds[c]
        r = jnp.where(inside, residual[c] + force[c], 0.0)
        d = r / centre
        for index in range(ITERS):
            v = v + d
            if index + 1 < ITERS:
                r = jnp.where(inside, r - apply(d), 0.0)
                rho_next = 1.0 / (2.0 * sigma - rho)
                d = rho_next * rho * d + 2.0 * rho_next / radius * r
                rho = rho_next
        velocity_out[c, :, :] = pltpu.roll(v, LANES - HALO, axis=1)[HALO : HALO + ROWS, 0:TILE]

    for copy in started:
        copy.wait_send()
    store.wait()


def per_device(fields, increments, velocity, geometry):
    hbm = pl.BlockSpec(memory_space=pltpu.HBM)

    def vmem(*shape):
        return pltpu.VMEM(shape, F32)

    return pl.pallas_call(
        kernel,
        out_shape=(
            jax.ShapeDtypeStruct(fields.shape, F32),
            jax.ShapeDtypeStruct(velocity.shape, F32),
        ),
        in_specs=[hbm] * 4,
        out_specs=(hbm, pl.BlockSpec(memory_space=pltpu.VMEM)),
        scratch_shapes=[
            vmem(3, LOCAL, TALL, (COLS + 2) * LANES),
            vmem(3, LOCAL, ROWS, COLS * LANES),
            vmem(2, ROWS, TILE),
            pltpu.VMEM((ROWS, COLS * LANES), jnp.int32),
            vmem(2, TALL, (COLS + 2) * LANES),
            vmem(2, 2, 3, COLS, LANES),
            vmem(3, COLS + 2, TALL, LANES),
            vmem(TILES, PACKED, LANES),
            vmem(8, LANES),
            vmem(TILES, 8, LANES),
            vmem(2, 16, LANES),
            vmem(2, 16, LANES),
            vmem(2, EDGE, COLS, LANES),
            vmem(2, EDGE, COLS, LANES),
            vmem(16, LANES),
            vmem(2, 16, LANES),
            vmem(RING, RING, ROWS, LANES),
            vmem(RING, 3, ROWS, LANES),
            vmem(3, ROWS, LANES),
            vmem(RING, ROWS, LANES),
            vmem(ROWS, LANES),
            vmem(2, TALL, LANES),
            vmem(2, 8, LANES),
            pltpu.SemaphoreType.DMA((9,)),
            pltpu.SemaphoreType.DMA((len(SLOTS),)),
            pltpu.SemaphoreType.DMA((len(SLOTS),)),
        ],
        compiler_params=pltpu.CompilerParams(
            collective_id=0, has_side_effects=True, vmem_limit_bytes=VMEM_LIMIT
        ),
        name="step",
    )(fields, increments, velocity, geometry)


def solution(mesh):
    placed = (
        P(None, "field", "space", None),
        P(None, "field", "space", None),
        P(None, "space", "field"),
        P("space", None),
    )
    return jax.shard_map(
        per_device,
        mesh=mesh,
        in_specs=placed,
        out_specs=(P(None, "field", "space", None), P(None, "space", "field")),
        check_vma=False,
    )
```

time: 67.6 us -> 62.9 us (0.930)
  local copies, waits for them, and re-layouts: 7.86 us -> 4.63 us
  Pallas kernels: 58.8 us -> 57.5 us
    unnamed x10 -> x4, local copies, waits for them, and re-layouts: 7.86 us -> 4.63 us
    pallas_call x1, Pallas kernels: 58.8 us -> 57.5 us  [per_device(): pl.pallas_call(kernel, out_shape=(jax.ShapeDtypeStruct(fields.shape, F32)...]
where the time goes in v2:
time: 62.9 us; the launch traced here: 62.8 us
  Pallas kernels  57.5 us (91%)
  local copies, waits for them, and re-layouts  4.63 us (7%)
  between operations  0.65 us (1%)
    pallas_call x1, Pallas kernels, per_device(): pl.pallas_call(kernel, out_shape=(jax.ShapeDtypeStruct(fields.shape, F32)...  57.5 us
    unnamed x4, local copies, waits for them, and re-layouts  4.63 us

profile of v2, /device:TPU:1, one launch (start us, length us, event | category | flops | bytes accessed | tf_op | source)
XLA Modules:
  0.0 62.8 jit_solution(9041765014848013326)
XLA Ops:
  0.6 57.5 %step.1 = (f32[3,4,64,1024]{3,2,1,0:T(8,128)}, f32[2,64,64]{2,1,0:T(8,128)}) custom-call(f32[3,4,64,1024]{3,2,1,0:T(8,128)} %fields.1, f32[3,4,64,1024]{3,2,1,0:T(8,128)} %noise.1, f32[2,64,64]{2,1,0:T(8,128)} %velocity.1, s32[64,1024]{1,0:T(8,128)} %geometry.1), custom_call_target="tpu_custom_call" | custom-call | tf_op jit(solution)/shard_map/step/pallas_call | solution.py:509
  58.2 0.0 copy-start
  58.2 4.0 %copy.8 = f32[3,4,64,1024]{3,2,1,0:T(8,128)} copy(f32[3,4,64,1024]{3,2,1,0:T(8,128)} %get-tuple-element.4) | data formatting | bytes 6291456
  62.2 0.0 copy-done
  62.2 0.6 %copy.9 = f32[2,64,64]{2,1,0:T(8,128)} copy(f32[2,64,64]{2,1,0:T(8,128)S(1)} %copy-done) | data formatting | bytes 65536
Async XLA Ops:
  58.2 4.0 %copy-start = (f32[2,64,64]{2,1,0:T(8,128)S(1)}, f32[2,64,64]{2,1,0:T(8,128)}, u32[]{:S(2)}) copy-start(f32[2,64,64]{2,1,0:T(8,128)} %get-tuple-element.5) | copy-start | bytes 98308

commit v3 on v2

--- a/solution.py
+++ b/solution.py
@@ -31,6 +31,8 @@
 LOCAL = 4
 VMEM_LIMIT = 63 * 1024 * 1024
 RING = 4
+CHUNKS = 2
+PIECE = ROWS // CHUNKS
 PACKED = 72
 EDGE = 12 * 3 + 1
 
@@ -38,8 +40,9 @@
 def slots():
     names = [(n, d) for n in ("max", "rim") for d in range(1, 16)]
     names += [(n, d) for n in ("vrow", "frow", "vcorner", "side", "end") for d in (0, 1)]
-    names += [(n, d) for n in ("z", "y") for d in (1, 2, 3)]
-    names += [("zy", o, d) for o in (1, 2, 3) for d in (1, 2, 3)]
+    names += [("y", d) for d in (1, 2, 3)]
+    names += [("z", o, h) for o in (1, 2, 3) for h in range(CHUNKS)]
+    names += [("zy", o, d, h) for o in (1, 2, 3) for d in (1, 2, 3) for h in range(CHUNKS)]
     names += [("part", j, d) for j in range(4) for d in (1, 2, 3)]
     names += [("sum", j) for j in range(3)]
     names += [("corner", a, b) for a in (0, 1) for b in (0, 1)]
@@ -56,28 +59,25 @@
     down_across = half_step * (u_right - u_left)
     across_down = half_step * (w_below - w_above)
     across_across = half_step * (w_right - w_left)
-    from_above = step * jnp.maximum(u, 0.0)
-    from_below = -step * jnp.minimum(u, 0.0)
-    from_left = step * jnp.maximum(w, 0.0)
-    from_right = -step * jnp.minimum(w, 0.0)
-    relaxed = step / RELAX
-    kept = 1.0 - relaxed - (from_above + from_below) - (from_left + from_right)
+    down, across = step * jnp.abs(u), step * jnp.abs(w)
+    relaxed = step * (1.0 / RELAX)
+    kept = 1.0 - relaxed - down - across
     own = (
         kept + 2.0 * down_down,
         kept + (down_down + across_across),
         kept + 2.0 * across_across,
     )
-    return own, (from_above, from_below, from_left, from_right), down_across, across_down, relaxed
+    return own, (u > 0.0, w > 0.0), (down, across), down_across, across_down, relaxed
 
 
 def update(weights, scale, tensors, noises):
-    own, sides, down_across, across_down, relaxed = weights
+    own, (downward, rightward), (down, across), down_across, across_down, relaxed = weights
     new = []
     for c in range(3):
-        value = own[c] * tensors[c][0] + scale * noises[c]
-        for side, beside in zip(sides, tensors[c][1:]):
-            value = value + side * beside
-        new.append(value)
+        here, above, below, left, right = tensors[c]
+        upwind = down * jnp.where(downward, above, below)
+        sidewind = across * jnp.where(rightward, left, right)
+        new.append((own[c] * here + scale * noises[c]) + (upwind + sidewind))
     xx, xy, yy = (tensor[0] for tensor in tensors)
     return (
         new[0] + (2.0 * down_across * xy + relaxed),
@@ -88,7 +88,7 @@
 
 def kernel(
     fields, noise, velocity, geometry, fields_out, velocity_out,
-    X, N, V, G, U, UE, S, PG, M_own, M_all, VR_out, VR_in, FE_out, FE_in, VC_out, VC_in,
+    XN, XC, XL, XR, N, V, G, U, UE, S, PG, M_own, M_all, VR_out, VR_in, FE_out, FE_in, VC_out, VC_in,
     Q, Y_in, Z_in, T, F, F_in, E_in, local_sem, send_sem, recv_sem,
 ):
     f = lax.axis_index("field")
@@ -138,8 +138,7 @@
     load_g.start()
     loads = []
     for c in range(3):
-        inner = X.at[c, :, HALO : HALO + ROWS, LANES : LANES + COLS * LANES]
-        loads.append(pltpu.make_async_copy(fields.at[c], inner, local_sem.at[2 + c]))
+        loads.append(pltpu.make_async_copy(fields.at[c], XN.at[c], local_sem.at[2 + c]))
     for c in range(3):
         loads.append(pltpu.make_async_copy(noise.at[c], N.at[c], local_sem.at[5 + c]))
     for copy in loads:
@@ -180,8 +179,10 @@
     pl.semaphore_wait(barrier, len(partners))
 
     main = PG.at[f, 0:ROWS]
-    for o in (2, 1, 3):
-        send(("z", o), main, main, z_peer(o), s)
+    for h in range(CHUNKS):
+        piece = PG.at[f, h * PIECE : (h + 1) * PIECE]
+        for o in (2, 1, 3):
+            send(("z", o, h), piece, piece, z_peer(o), s)
     for d in (2, 1, 3):
         send(("y", d), main, main, y_peer(d), s)
     send(("vrow", 0), VR_out.at[0], VR_in.at[0], f, s_up)
@@ -193,15 +194,14 @@
         copy.wait()
     for t in range(COLS):
         columns = slice(t * LANES, (t + 1) * LANES)
-        inner = slice((t + 1) * LANES, (t + 2) * LANES)
         here = slice(t, t + 1)
         for c in range(3):
             for e in range(LOCAL):
                 at = c * LOCAL + e
                 for side, edge, step in ((0, ROWS - 1, -1), (1, 0, 1)):
-                    near = HALO + edge
-                    FE_out[side, at, here, :] = X[c, e, near : near + 1, inner]
-                    FE_out[side, 12 + at, here, :] = X[c, e, near + step : near + step + 1, inner]
+                    second = edge + step
+                    FE_out[side, at, here, :] = XN[c, e, edge : edge + 1, columns]
+                    FE_out[side, 12 + at, here, :] = XN[c, e, second : second + 1, columns]
                     FE_out[side, 24 + at, here, :] = N[c, e, edge : edge + 1, columns]
         for side, edge in ((0, ROWS - 1), (1, 0)):
             FE_out[side, EDGE - 1, here, :] = G[edge : edge + 1, columns].astype(F32)
@@ -224,21 +224,37 @@
     for d in range(1, TILES):
         send(("rim", d), rim, rim, (f + d) % TILES, s)
 
-    for o in (1, 3, 2):
-        tile = PG.at[peer_back(o, 0), 0:ROWS]
-        arrive(("z", o), tile)
-        for d in (2, 1, 3):
-            send(("zy", o, d), tile, tile, y_peer(d), s)
+    for h in range(CHUNKS):
+        for o in (1, 3, 2):
+            piece = PG.at[peer_back(o, 0), h * PIECE : (h + 1) * PIECE]
+            arrive(("z", o, h), piece)
+            for d in (2, 1, 3):
+                send(("zy", o, d, h), piece, piece, y_peer(d), s)
     VC_out[0:8, :] = VR_in[0, 0:8, :]
     VC_out[8:16, :] = VR_in[1, 0:8, :]
     send(("vcorner", 0), VC_out, VC_in.at[0], f_up, s)
     send(("vcorner", 1), VC_out, VC_in.at[1], f_down, s)
 
-    for c in range(3):
-        for e in range(LOCAL):
-            for t in (0, COLS + 1):
-                outer = slice(t * LANES, (t + 1) * LANES)
-                X[c, e, :, outer] = jnp.full((TALL, LANES), float(c != 1), F32)
+    def block_at(t):
+        return pl.ds(pl.multiple_of(t * LANES, LANES), LANES)
+
+    def prepare(i, carry):
+        t, r = i // 8, i % 8
+        rows, rows_in = pl.ds(pl.multiple_of(r * 8, 8), 8), pl.ds(pl.multiple_of(r * 8 + HALO, 8), 8)
+        here_at, before_at = block_at(t), block_at(jnp.maximum(t - 1, 0))
+        after_at = block_at(jnp.minimum(t + 1, COLS - 1))
+        for c in range(3):
+            outside = float(c != 1)
+            for e in range(LOCAL):
+                here = XN[c, e, rows, here_at]
+                before = jnp.where(t == 0, outside, XN[c, e, rows, before_at])
+                after = jnp.where(t == COLS - 1, outside, XN[c, e, rows, after_at])
+                XC[c, e, t, rows_in, :] = here
+                XL[c, e, t, rows, :] = pltpu.roll(jnp.where(at_right, before, here), 1, axis=1)
+                XR[c, e, t, rows, :] = pltpu.roll(jnp.where(at_left, after, here), LANES - 1, axis=1)
+        return carry
+
+    lax.fori_loop(0, 64, prepare, 0)
     for t in (0, COLS + 1):
         U[:, :, t * LANES : (t + 1) * LANES] = jnp.zeros((2, TALL, LANES), F32)
         S[:, t, :, :] = jnp.zeros((3, TALL, LANES), F32)
@@ -250,15 +266,15 @@
             row_above = jnp.where(first, outside, FE_in[0, c * LOCAL + e])
             row_below = jnp.where(last, outside, FE_in[1, c * LOCAL + e])
             for t in range(COLS):
-                inner = slice((t + 1) * LANES, (t + 2) * LANES)
-                X[c, e, HALO - 1 : HALO, inner] = row_above[t : t + 1]
-                X[c, e, HALO + ROWS : HALO + ROWS + 1, inner] = row_below[t : t + 1]
+                XC[c, e, t, HALO - 1 : HALO, :] = row_above[t : t + 1]
+                XC[c, e, t, HALO + ROWS : HALO + ROWS + 1, :] = row_below[t : t + 1]
 
     for d in (1, 2, 3):
         arrive(("y", d), PG.at[peer_back(0, d), 0:ROWS])
     for o in (1, 3, 2):
         for d in (1, 2, 3):
-            arrive(("zy", o, d), PG.at[peer_back(o, d), 0:ROWS])
+            for h in range(CHUNKS):
+                arrive(("zy", o, d, h), PG.at[peer_back(o, d), h * PIECE : (h + 1) * PIECE])
     for d in range(1, TILES):
         arrive(("rim", d), PG.at[(f + TILES - d) % TILES, ROWS:PACKED])
 
@@ -323,9 +339,6 @@
             for t in range(COLS):
                 S[c, t + 1, place : place + 1, :] = values[t : t + 1]
 
-    def block_at(t):
-        return pl.ds(pl.multiple_of(t * LANES, LANES), LANES)
-
     def nearby(ref, lead, r, t):
         rows, columns = pl.ds(pl.multiple_of(r * 8 + HALO, 8), 8), block_at(t)
         rows_above = pl.ds(pl.multiple_of(r * 8, 8), 8)
@@ -346,48 +359,61 @@
     start = 2 * ((zh + 1) % RING) + COLS - 1
 
     def advance(i, carry):
-        t = (start + i // 8) % COLS + 1
-        r = i % 8
-        rows, columns = pl.ds(pl.multiple_of(r * 8, 8), 8), block_at(t - 1)
-        weights = coefficients(step, nearby(U, (0,), r, t), nearby(U, (1,), r, t))
-        total = None
-        for e in range(LOCAL):
-            tensors = [nearby(X, (c, e), r, t) for c in range(3)]
-            noises = [N[c, e, rows, columns] for c in range(3)]
-            new = update(weights, scale, tensors, noises)
-            for c in range(3):
-                N[c, e, rows, columns] = new[c]
-            total = added(total, new)
-        weight = G[rows, columns].astype(F32)
-        for c, values in enumerate(stress_of(total, weight)):
-            S[c, t, pl.ds(pl.multiple_of(r * 8 + HALO, 8), 8), :] = values
+        t = (start + i // 4) % COLS
+        for part in (0, 1):
+            r = i % 4 * 2 + part
+            rows, columns = pl.ds(pl.multiple_of(r * 8, 8), 8), block_at(t)
+            rows_in = pl.ds(pl.multiple_of(r * 8 + HALO, 8), 8)
+            rows_above, rows_below = pl.ds(r * 8 + HALO - 1, 8), pl.ds(r * 8 + HALO + 1, 8)
+            weights = coefficients(step, nearby(U, (0,), r, t + 1), nearby(U, (1,), r, t + 1))
+            total = None
+            for e in range(LOCAL):
+                tensors = [
+                    (
+                        XC[c, e, t, rows_in, :],
+                        XC[c, e, t, rows_above, :],
+                        XC[c, e, t, rows_below, :],
+                        XL[c, e, t, rows, :],
+                        XR[c, e, t, rows, :],
+                    )
+                    for c in range(3)
+                ]
+                noises = [N[c, e, rows, columns] for c in range(3)]
+                new = update(weights, scale, tensors, noises)
+                for c in range(3):
+                    N[c, e, rows, columns] = new[c]
+                total = added(total, new)
+            weight = G[rows, columns].astype(F32)
+            for c, values in enumerate(stress_of(total, weight)):
+                S[c, t + 1, rows_in, :] = values
         return carry
 
     def forces(j):
         block = (zh + 1 + j) % RING
 
-        def body(i, carry):
-            tt, r = i // 8, i % 8
+        def body(tt, carry):
             t = 2 * block + tt + 1
-            rows = pl.ds(pl.multiple_of(r * 8 + HALO, 8), 8)
-
-            def along_rows(c):
-                return S[c, t, pl.ds(r * 8 + HALO + 1, 8), :] - S[c, t, pl.ds(r * 8 + HALO - 1, 8), :]
-
-            def along_cols(c):
-                here = S[c, t, rows, :]
-                left = jnp.where(at_right, S[c, t - 1, rows, :], here)
-                right = jnp.where(at_left, S[c, t + 1, rows, :], here)
-                return pltpu.roll(right, LANES - 1, axis=1) - pltpu.roll(left, 1, axis=1)
-
-            down = 0.5 * (along_rows(0) + along_cols(1))
-            across = 0.5 * (along_rows(1) + along_cols(2))
-            rows = pl.ds(pl.multiple_of(r * 8, 8), 8)
-            Q[j, 2 * tt, rows, :] = jnp.where(low, down, pltpu.roll(across, TILE, axis=1))
-            Q[j, 2 * tt + 1, rows, :] = jnp.where(low, pltpu.roll(down, TILE, axis=1), across)
+            for r in range(ROWS // 8):
+                top = r * 8 + HALO
+                rows = slice(top, top + 8)
+
+                def along_rows(c):
+                    return S[c, t, top + 1 : top + 9, :] - S[c, t, top - 1 : top + 7, :]
+
+                def along_cols(c):
+                    here = S[c, t, rows, :]
+                    left = jnp.where(at_right, S[c, t - 1, rows, :], here)
+                    right = jnp.where(at_left, S[c, t + 1, rows, :], here)
+                    return pltpu.roll(right, LANES - 1, axis=1) - pltpu.roll(left, 1, axis=1)
+
+                down = 0.5 * (along_rows(0) + along_cols(1))
+                across = 0.5 * (along_rows(1) + along_cols(2))
+                packed = slice(r * 8, r * 8 + 8)
+                Q[j, 2 * tt, packed, :] = jnp.where(low, down, pltpu.roll(across, TILE, axis=1))
+                Q[j, 2 * tt + 1, packed, :] = jnp.where(low, pltpu.roll(down, TILE, axis=1), across)
             return carry
 
-        lax.fori_loop(0, 16, body, 0)
+        lax.fori_loop(0, 2, body, 0)
         for d in (2, 1, 3):
             send(("part", j, d), Q.at[j, (y + d) % RING], Y_in.at[j, d - 1], y_peer(d), s)
 
@@ -398,11 +424,11 @@
         if j < 3:
             send(("sum", j), T.at[j], Z_in.at[j], z_peer(j + 1), s)
 
-    lax.fori_loop(0, 32, advance, 0)
+    lax.fori_loop(0, 16, advance, 0)
     forces(0)
-    lax.fori_loop(32, 48, advance, 0)
+    lax.fori_loop(16, 24, advance, 0)
     forces(1)
-    lax.fori_loop(48, 64, advance, 0)
+    lax.fori_loop(24, 32, advance, 0)
     forces(2)
     forces(3)
     store = pltpu.make_async_copy(N, fields_out, local_sem.at[8])
@@ -515,7 +541,10 @@
         in_specs=[hbm] * 4,
         out_specs=(hbm, pl.BlockSpec(memory_space=pltpu.VMEM)),
         scratch_shapes=[
-            vmem(3, LOCAL, TALL, (COLS + 2) * LANES),
+            vmem(3, LOCAL, ROWS, COLS * LANES),
+            vmem(3, LOCAL, COLS, TALL, LANES),
+            vmem(3, LOCAL, COLS, ROWS, LANES),
+            vmem(3, LOCAL, COLS, ROWS, LANES),
             vmem(3, LOCAL, ROWS, COLS * LANES),
             vmem(2, ROWS, TILE),
             pltpu.VMEM((ROWS, COLS * LANES), jnp.int32),

time: 62.9 us -> 53.7 us (0.85)
  Pallas kernels: 57.5 us -> 48.3 us
    pallas_call x1, Pallas kernels: 57.5 us -> 48.3 us  [per_device(): pl.pallas_call(kernel, out_shape=(jax.ShapeDtypeStruct(fields.shape, F32)...]
where the time goes in v3:
time: 53.7 us; the launch traced here: 53.6 us
  Pallas kernels  48.3 us (90%)
  local copies, waits for them, and re-layouts  4.63 us (9%)
  between operations  0.65 us (1%)
    pallas_call x1, Pallas kernels, per_device(): pl.pallas_call(kernel, out_shape=(jax.ShapeDtypeStruct(fields.shape, F32)...  48.3 us
    unnamed x4, local copies, waits for them, and re-layouts  4.63 us

profile of v3, /device:TPU:1, one launch (start us, length us, event | category | flops | bytes accessed | tf_op | source)
XLA Modules:
  0.0 53.6 jit_solution(949465857536187849)
XLA Ops:
  0.6 48.3 %step.1 = (f32[3,4,64,1024]{3,2,1,0:T(8,128)}, f32[2,64,64]{2,1,0:T(8,128)}) custom-call(f32[3,4,64,1024]{3,2,1,0:T(8,128)} %fields.1, f32[3,4,64,1024]{3,2,1,0:T(8,128)} %noise.1, f32[2,64,64]{2,1,0:T(8,128)} %velocity.1, s32[64,1024]{1,0:T(8,128)} %geometry.1), custom_call_target="tpu_custom_call" | custom-call | tf_op jit(solution)/shard_map/step/pallas_call | solution.py:535
  49.0 0.0 copy-start
  49.0 4.0 %copy.8 = f32[3,4,64,1024]{3,2,1,0:T(8,128)} copy(f32[3,4,64,1024]{3,2,1,0:T(8,128)} %get-tuple-element.4) | data formatting | bytes 6291456
  53.0 0.0 copy-done
  53.0 0.6 %copy.9 = f32[2,64,64]{2,1,0:T(8,128)} copy(f32[2,64,64]{2,1,0:T(8,128)S(1)} %copy-done) | data formatting | bytes 65536
Async XLA Ops:
  49.0 4.0 %copy-start = (f32[2,64,64]{2,1,0:T(8,128)S(1)}, f32[2,64,64]{2,1,0:T(8,128)}, u32[]{:S(2)}) copy-start(f32[2,64,64]{2,1,0:T(8,128)} %get-tuple-element.5) | copy-start | bytes 98308

commit v4 on v3

--- a/solution.py
+++ b/solution.py
@@ -39,13 +39,14 @@
 
 def slots():
     names = [(n, d) for n in ("max", "rim") for d in range(1, 16)]
-    names += [(n, d) for n in ("vrow", "frow", "vcorner", "side", "end") for d in (0, 1)]
+    names += [(n, d) for n in ("vrow", "frow", "vcorner") for d in (0, 1)]
     names += [("y", d) for d in (1, 2, 3)]
     names += [("z", o, h) for o in (1, 2, 3) for h in range(CHUNKS)]
     names += [("zy", o, d, h) for o in (1, 2, 3) for d in (1, 2, 3) for h in range(CHUNKS)]
     names += [("part", j, d) for j in range(4) for d in (1, 2, 3)]
     names += [("sum", j) for j in range(3)]
-    names += [("corner", a, b) for a in (0, 1) for b in (0, 1)]
+    names += [(n, d, j) for n in ("side", "end") for d in (0, 1) for j in range(4)]
+    names += [("corner", a, b, j) for a in (0, 1) for b in (0, 1) for j in range(4)]
     return {name: at for at, name in enumerate(names)}
 
 
@@ -89,7 +90,7 @@
 def kernel(
     fields, noise, velocity, geometry, fields_out, velocity_out,
     XN, XC, XL, XR, N, V, G, U, UE, S, PG, M_own, M_all, VR_out, VR_in, FE_out, FE_in, VC_out, VC_in,
-    Q, Y_in, Z_in, T, F, F_in, E_in, local_sem, send_sem, recv_sem,
+    Q, Y_in, Z_in, T, C, C_in, E_in, K_in, local_sem, send_sem, recv_sem,
 ):
     f = lax.axis_index("field")
     s = lax.axis_index("space")
@@ -128,7 +129,10 @@
     barrier = pltpu.get_barrier_semaphore()
     partners = [(f, (s + d) % TILES) for d in range(1, TILES)]
     partners += [((f + d) % TILES, s) for d in range(1, TILES)]
-    partners += [(a, b) for a in (f_up, f_down) for b in (s_up, s_down)]
+    partners += [(z_peer(o), b) for o in (1, 2, 3) for b in (s_up, s_down)]
+    partners += [
+        ((z_peer(o) + a) % TILES, b) for o in range(4) for a in (1, TILES - 1) for b in (s_up, s_down)
+    ]
     for partner in partners:
         pl.semaphore_signal(barrier, inc=1, device_id=partner, device_id_type=MESH)
 
@@ -178,6 +182,10 @@
 
     pl.semaphore_wait(barrier, len(partners))
 
+    send(("vrow", 0), VR_out.at[0], VR_in.at[0], f, s_up)
+    send(("vrow", 1), VR_out.at[1], VR_in.at[1], f, s_down)
+    for d in range(1, TILES):
+        send(("max", d), M_own, M_all.at[d], f, (s + d) % TILES)
     main = PG.at[f, 0:ROWS]
     for h in range(CHUNKS):
         piece = PG.at[f, h * PIECE : (h + 1) * PIECE]
@@ -185,10 +193,6 @@
             send(("z", o, h), piece, piece, z_peer(o), s)
     for d in (2, 1, 3):
         send(("y", d), main, main, y_peer(d), s)
-    send(("vrow", 0), VR_out.at[0], VR_in.at[0], f, s_up)
-    send(("vrow", 1), VR_out.at[1], VR_in.at[1], f, s_down)
-    for d in range(1, TILES):
-        send(("max", d), M_own, M_all.at[d], f, (s + d) % TILES)
 
     for copy in loads:
         copy.wait()
@@ -417,12 +421,38 @@
         for d in (2, 1, 3):
             send(("part", j, d), Q.at[j, (y + d) % RING], Y_in.at[j, d - 1], y_peer(d), s)
 
+    wide_lane = lax.broadcasted_iota(jnp.int32, (ROWS, LANES), 1)
+
+    def edges(tile):
+        turned = pltpu.roll(tile, HALO + TILE, axis=1)
+        for wide in (
+            jnp.where(wide_lane < 8, turned, pltpu.roll(tile, 16, axis=1)),
+            jnp.where(wide_lane < 8, tile, turned),
+        ):
+            folded = wide[0:8]
+            for block in range(1, 8):
+                part = pltpu.roll(wide[8 * block : 8 * block + 8], 16 * block, axis=1)
+                folded = jnp.where(lane >= 16 * block, part, folded)
+            yield folded
+
     def ring_sum(j):
+        owner = z_peer(j + 1)
+        neighbours = (0, (owner + 1) % TILES), (1, (owner + TILES - 1) % TILES)
         for d in (1, 2, 3):
             arrive(("part", j, d), Y_in.at[j, d - 1])
-        T[j] = (Q[j, y] + Y_in[j, 0]) + (Y_in[j, 1] + Y_in[j, 2])
+        tile = (Q[j, y] + Y_in[j, 0]) + (Y_in[j, 1] + Y_in[j, 2])
+        T[j] = tile
+        ends = (0, s_up, T.at[j, ROWS - 8 : ROWS]), (1, s_down, T.at[j, 0:8])
+        for b, to_s, rows in ends:
+            for a, to_f in neighbours:
+                send(("corner", a, b, j), rows, K_in.at[a, b, j], to_f, to_s)
         if j < 3:
-            send(("sum", j), T.at[j], Z_in.at[j], z_peer(j + 1), s)
+            send(("sum", j), T.at[j], Z_in.at[j], owner, s)
+        for b, to_s, rows in ends:
+            send(("end", b, j), rows, E_in.at[b, j], owner, to_s)
+        for (a, to_f), edge in zip(neighbours, edges(tile)):
+            C[j, a] = edge
+            send(("side", a, j), C.at[j, a], C_in.at[a, j], to_f, s)
 
     lax.fori_loop(0, 16, advance, 0)
     forces(0)
@@ -445,24 +475,22 @@
     for d in (0, 1):
         arrive(("vcorner", d), VC_in.at[d])
 
-    def windows(before, here, after):
-        near = lambda v: pltpu.roll(v, HALO, axis=1)
-        far = lambda v: pltpu.roll(v, HALO + TILE, axis=1)
-
-        def window(a, b, c):
-            joined = jnp.where(at_lane < HALO, a, jnp.where(at_lane < HALO + TILE, b, c))
-            return jnp.where(inside, joined, 0.0)
-
-        return (
-            window(far(before), near(here), far(after)),
-            window(near(before), far(here), near(after)),
-        )
+    near = lambda values: pltpu.roll(values, HALO, axis=1)
+    far = lambda values: pltpu.roll(values, HALO + TILE, axis=1)
+
+    def window(before, here, after):
+        joined = jnp.where(at_lane < HALO, before, jnp.where(at_lane < HALO + TILE, here, after))
+        return jnp.where(inside, joined, 0.0)
 
     def stacked(rim_rows, tile):
         return jnp.concatenate([rim_rows[0:8], PG[tile, 0:ROWS, :], rim_rows[8:16]], axis=0)
 
-    speeds = windows(
+    v_before, v_here, v_after = (
         stacked(VC_in.at[0], f_down), stacked(VC_out, f), stacked(VC_in.at[1], f_up)
+    )
+    speeds = (
+        window(far(v_before), near(v_here), far(v_after)),
+        window(near(v_before), far(v_here), near(v_after)),
     )
     mask = jnp.concatenate([VR_in[0, 8:16, :], walls(slice(0, ROWS)), VR_in[1, 8:16, :]], axis=0)
     weight = BETA + 4.0 * VISCOSITY + PENALTY * (1.0 - mask)
@@ -483,26 +511,37 @@
     for j in range(3):
         arrive(("sum", j), Z_in.at[j])
         total = total + Z_in[j]
-    F[...] = total
-    for b, to_s in ((0, s_up), (1, s_down)):
-        rows = slice(ROWS - 8, ROWS) if b == 0 else slice(0, 8)
-        landing = slice(0, 8) if b == 0 else slice(HALO + ROWS, TALL)
-        for a, to_f in ((0, f_up), (1, f_down)):
-            send(("corner", a, b), F.at[rows], F_in.at[a, landing], to_f, to_s)
-    for a, to_f in ((0, f_up), (1, f_down)):
-        send(("side", a), F, F_in.at[a, HALO : HALO + ROWS], to_f, s)
-    for b, to_s in ((0, s_up), (1, s_down)):
-        rows = slice(ROWS - 8, ROWS) if b == 0 else slice(0, 8)
-        send(("end", b), F.at[rows], E_in.at[b], f, to_s)
-    for b in (0, 1):
-        arrive(("end", b), E_in.at[b])
-    for a in (0, 1):
-        arrive(("side", a), F_in.at[a, HALO : HALO + ROWS])
-    for b in (0, 1):
+    for j in range(4):
+        for b in (0, 1):
+            for a in (0, 1):
+                arrive(("corner", a, b, j), K_in.at[a, b, j])
+            arrive(("end", b, j), E_in.at[b, j])
         for a in (0, 1):
-            landing = slice(0, 8) if b == 0 else slice(HALO + ROWS, TALL)
-            arrive(("corner", a, b), F_in.at[a, landing])
-    force = windows(F_in[0], jnp.concatenate([E_in[0], F[...], E_in[1]], axis=0), F_in[1])
+            arrive(("side", a, j), C_in.at[a, j])
+
+    def summed(ref, *lead):
+        return (ref[(*lead, 0)] + ref[(*lead, 1)]) + (ref[(*lead, 2)] + ref[(*lead, 3)])
+
+    def beside(a, turn, first, second):
+        folded = summed(C_in, a)
+        corners = [summed(K_in, a, b) for b in (0, 1)]
+        return tuple(
+            jnp.concatenate(
+                [place(corners[0])]
+                + [pltpu.roll(folded, (turn - 16 * block - 8 * c) % LANES, axis=1) for block in range(8)]
+                + [place(corners[1])],
+                axis=0,
+            )
+            for c, place in enumerate((first, second))
+        )
+
+    f_before = beside(0, 0, far, near)
+    f_after = beside(1, HALO + TILE, far, near)
+    f_here = jnp.concatenate([summed(E_in, 0), total, summed(E_in, 1)], axis=0)
+    force = (
+        window(f_before[0], near(f_here), f_after[0]),
+        window(f_before[1], far(f_here), f_after[1]),
+    )
 
     centre = 0.5 * (UPPER + LOWER)
     radius = 0.5 * (UPPER - LOWER)
@@ -564,9 +603,10 @@
             vmem(RING, 3, ROWS, LANES),
             vmem(3, ROWS, LANES),
             vmem(RING, ROWS, LANES),
-            vmem(ROWS, LANES),
-            vmem(2, TALL, LANES),
-            vmem(2, 8, LANES),
+            vmem(RING, 2, 8, LANES),
+            vmem(2, RING, 8, LANES),
+            vmem(2, RING, 8, LANES),
+            vmem(2, 2, RING, 8, LANES),
             pltpu.SemaphoreType.DMA((9,)),
             pltpu.SemaphoreType.DMA((len(SLOTS),)),
             pltpu.SemaphoreType.DMA((len(SLOTS),)),

time: 53.7 us -> 51 us (0.950)
  Pallas kernels: 48.3 us -> 45.6 us
    pallas_call x1, Pallas kernels: 48.3 us -> 45.6 us  [per_device(): pl.pallas_call(kernel, out_shape=(jax.ShapeDtypeStruct(fields.shape, F32)...]
where the time goes in v4:
time: 51 us; the launch traced here: 50.9 us
  Pallas kernels  45.6 us (89%)
  local copies, waits for them, and re-layouts  4.63 us (9%)
  between operations  0.65 us (1%)
    pallas_call x1, Pallas kernels, per_device(): pl.pallas_call(kernel, out_shape=(jax.ShapeDtypeStruct(fields.shape, F32)...  45.6 us
    unnamed x4, local copies, waits for them, and re-layouts  4.63 us

profile of v4, /device:TPU:1, one launch (start us, length us, event | category | flops | bytes accessed | tf_op | source)
XLA Modules:
  0.0 50.9 jit_solution(9353432074493647673)
XLA Ops:
  0.6 45.6 %step.1 = (f32[3,4,64,1024]{3,2,1,0:T(8,128)}, f32[2,64,64]{2,1,0:T(8,128)}) custom-call(f32[3,4,64,1024]{3,2,1,0:T(8,128)} %fields.1, f32[3,4,64,1024]{3,2,1,0:T(8,128)} %noise.1, f32[2,64,64]{2,1,0:T(8,128)} %velocity.1, s32[64,1024]{1,0:T(8,128)} %geometry.1), custom_call_target="tpu_custom_call" | custom-call | tf_op jit(solution)/shard_map/step/pallas_call | solution.py:574
  46.2 0.0 copy-start
  46.2 4.0 %copy.8 = f32[3,4,64,1024]{3,2,1,0:T(8,128)} copy(f32[3,4,64,1024]{3,2,1,0:T(8,128)} %get-tuple-element.4) | data formatting | bytes 6291456
  50.2 0.0 copy-done
  50.2 0.6 %copy.9 = f32[2,64,64]{2,1,0:T(8,128)} copy(f32[2,64,64]{2,1,0:T(8,128)S(1)} %copy-done) | data formatting | bytes 65536
Async XLA Ops:
  46.2 4.0 %copy-start = (f32[2,64,64]{2,1,0:T(8,128)S(1)}, f32[2,64,64]{2,1,0:T(8,128)}, u32[]{:S(2)}) copy-start(f32[2,64,64]{2,1,0:T(8,128)} %get-tuple-element.5) | copy-start | bytes 98308

commit v5 on v4

--- a/solution.py
+++ b/solution.py
@@ -38,7 +38,8 @@
 
 
 def slots():
-    names = [(n, d) for n in ("max", "rim") for d in range(1, 16)]
+    names = [(n, d) for n in ("max",) for d in range(1, 16)]
+    names += [("rim", o, d) for o in range(4) for d in range(4) if o or d]
     names += [(n, d) for n in ("vrow", "frow", "vcorner") for d in (0, 1)]
     names += [("y", d) for d in (1, 2, 3)]
     names += [("z", o, h) for o in (1, 2, 3) for h in range(CHUNKS)]
@@ -128,11 +129,7 @@
 
     barrier = pltpu.get_barrier_semaphore()
     partners = [(f, (s + d) % TILES) for d in range(1, TILES)]
-    partners += [((f + d) % TILES, s) for d in range(1, TILES)]
-    partners += [(z_peer(o), b) for o in (1, 2, 3) for b in (s_up, s_down)]
-    partners += [
-        ((z_peer(o) + a) % TILES, b) for o in range(4) for a in (1, TILES - 1) for b in (s_up, s_down)
-    ]
+    partners += [(y_peer(d), s) for d in (1, 2, 3)] + [(z_peer(d), s) for d in (1, 2, 3)]
     for partner in partners:
         pl.semaphore_signal(barrier, inc=1, device_id=partner, device_id_type=MESH)
 
@@ -225,8 +222,13 @@
     PG[f, ROWS + 2 : ROWS + 4, :] = below
     PG[f, ROWS + 4 : PACKED, :] = jnp.broadcast_to(speed, (PACKED - ROWS - 4, LANES))
     rim = PG.at[f, ROWS:PACKED]
-    for d in range(1, TILES):
-        send(("rim", d), rim, rim, (f + d) % TILES, s)
+
+    def send_rim(o, d):
+        send(("rim", o, d), rim, rim, (zh + o) % RING * RING + (y + d) % RING, s)
+
+    for at in (1, 2, 3):
+        send_rim(at, 0)
+        send_rim(0, at)
 
     for h in range(CHUNKS):
         for o in (1, 3, 2):
@@ -234,6 +236,9 @@
             arrive(("z", o, h), piece)
             for d in (2, 1, 3):
                 send(("zy", o, d, h), piece, piece, y_peer(d), s)
+            if h == 0:
+                for d in (2, 1, 3):
+                    send_rim(RING - o, d)
     VC_out[0:8, :] = VR_in[0, 0:8, :]
     VC_out[8:16, :] = VR_in[1, 0:8, :]
     send(("vcorner", 0), VC_out, VC_in.at[0], f_up, s)
@@ -273,34 +278,39 @@
                 XC[c, e, t, HALO - 1 : HALO, :] = row_above[t : t + 1]
                 XC[c, e, t, HALO + ROWS : HALO + ROWS + 1, :] = row_below[t : t + 1]
 
-    for d in (1, 2, 3):
-        arrive(("y", d), PG.at[peer_back(0, d), 0:ROWS])
-    for o in (1, 3, 2):
-        for d in (1, 2, 3):
-            for h in range(CHUNKS):
-                arrive(("zy", o, d, h), PG.at[peer_back(o, d), h * PIECE : (h + 1) * PIECE])
-    for d in range(1, TILES):
-        arrive(("rim", d), PG.at[(f + TILES - d) % TILES, ROWS:PACKED])
-
     low_tile = lax.broadcasted_iota(jnp.int32, (PACKED, LANES), 1) < TILE
     speed = jnp.zeros((1, LANES), F32)
+    for o in range(4):
+        for d in range(4):
+            if o or d:
+                arrive(("rim", o, d), PG.at[peer_back(o, d), ROWS:PACKED])
+    for o in (0, 1, 3, 2):
+        for d in (1, 2, 3):
+            if o == 0:
+                arrive(("y", d), PG.at[peer_back(0, d), 0:ROWS])
+            else:
+                for h in range(CHUNKS):
+                    arrive(("zy", o, d, h), PG.at[peer_back(o, d), h * PIECE : (h + 1) * PIECE])
+        for tt in (0, 1):
+            t = (zh + RING - o) % RING * 2 + tt
+            even, odd = PG[2 * t], PG[2 * t + 1]
+            u = jnp.where(low_tile, even, pltpu.roll(odd, TILE, axis=1))
+            w = jnp.where(low_tile, pltpu.roll(even, TILE, axis=1), odd)
+            columns = block_at(t + 1)
+            for c, strip in ((0, u), (1, w)):
+                U[c, HALO : HALO + ROWS, columns] = strip[0:ROWS]
+                U[c, HALO - 2 : HALO, columns] = strip[ROWS : ROWS + 2]
+                U[c, HALO + ROWS : HALO + ROWS + 2, columns] = strip[ROWS + 2 : ROWS + 4]
+            speed = jnp.maximum(
+                speed, jnp.maximum(even[ROWS + 4 : ROWS + 5], odd[ROWS + 4 : ROWS + 5])
+            )
     for t in range(COLS):
-        even, odd = PG[2 * t], PG[2 * t + 1]
-        u = jnp.where(low_tile, even, pltpu.roll(odd, TILE, axis=1))
-        w = jnp.where(low_tile, pltpu.roll(even, TILE, axis=1), odd)
         columns = slice((t + 1) * LANES, (t + 2) * LANES)
         here = slice(t, t + 1)
-        for c, strip in ((0, u), (1, w)):
-            U[c, HALO : HALO + ROWS, columns] = strip[0:ROWS]
-            U[c, HALO - 2 : HALO, columns] = strip[ROWS : ROWS + 2]
-            U[c, HALO + ROWS : HALO + ROWS + 2, columns] = strip[ROWS + 2 : ROWS + 4]
-            UE[0, c, 0, here, :] = strip[ROWS + 1 : ROWS + 2]
-            UE[0, c, 1, here, :] = strip[ROWS : ROWS + 1]
-            UE[0, c, 2, here, :] = strip[0:1]
-            UE[1, c, 0, here, :] = strip[ROWS + 2 : ROWS + 3]
-            UE[1, c, 1, here, :] = strip[ROWS - 1 : ROWS]
-            UE[1, c, 2, here, :] = strip[ROWS + 3 : ROWS + 4]
-        speed = jnp.maximum(speed, jnp.maximum(even[ROWS + 4 : ROWS + 5], odd[ROWS + 4 : ROWS + 5]))
+        for c in range(2):
+            for side, rows in ((0, (HALO - 1, HALO - 2, HALO)), (1, (HALO + ROWS, HALO + ROWS - 1, HALO + ROWS + 1))):
+                for q, at in enumerate(rows):
+                    UE[side, c, q, here, :] = U[c, at : at + 1, columns]
     speed = jnp.max(speed, axis=1, keepdims=True)
     step = COURANT / (speed + SPEED_EPS)
     step = jnp.broadcast_to(step, (8, LANES))
@@ -463,10 +473,6 @@
     forces(3)
     store = pltpu.make_async_copy(N, fields_out, local_sem.at[8])
     store.start()
-    ring_sum(0)
-    ring_sum(1)
-    ring_sum(2)
-
     at_row = lax.broadcasted_iota(jnp.int32, (TALL, LANES), 0) + (s * ROWS - HALO)
     at_lane = lax.broadcasted_iota(jnp.int32, (TALL, LANES), 1)
     at_col = at_lane + (f * TILE - HALO)
@@ -506,6 +512,9 @@
 
     residual = [BETA * v - apply(v) for v in speeds]
 
+    ring_sum(0)
+    ring_sum(1)
+    ring_sum(2)
     ring_sum(3)
     total = T[3]
     for j in range(3):

time: 51 us -> 48.8 us (0.957)
  Pallas kernels: 45.6 us -> 43.4 us
    pallas_call x1, Pallas kernels: 45.6 us -> 43.4 us  [per_device(): pl.pallas_call(kernel, out_shape=(jax.ShapeDtypeStruct(fields.shape, F32)...]
where the time goes in v5:
time: 48.8 us; the launch traced here: 48.7 us
  Pallas kernels  43.4 us (89%)
  local copies, waits for them, and re-layouts  4.63 us (9%)
  between operations  0.65 us (1%)
    pallas_call x1, Pallas kernels, per_device(): pl.pallas_call(kernel, out_shape=(jax.ShapeDtypeStruct(fields.shape, F32)...  43.4 us
    unnamed x4, local copies, waits for them, and re-layouts  4.63 us

profile of v5, /device:TPU:1, one launch (start us, length us, event | category | flops | bytes accessed | tf_op | source)
XLA Modules:
  0.0 48.7 jit_solution(9549954109315052808)
XLA Ops:
  0.6 43.4 %step.1 = (f32[3,4,64,1024]{3,2,1,0:T(8,128)}, f32[2,64,64]{2,1,0:T(8,128)}) custom-call(f32[3,4,64,1024]{3,2,1,0:T(8,128)} %fields.1, f32[3,4,64,1024]{3,2,1,0:T(8,128)} %noise.1, f32[2,64,64]{2,1,0:T(8,128)} %velocity.1, s32[64,1024]{1,0:T(8,128)} %geometry.1), custom_call_target="tpu_custom_call" | custom-call | tf_op jit(solution)/shard_map/step/pallas_call | solution.py:583
  44.1 0.0 copy-start
  44.1 4.0 %copy.8 = f32[3,4,64,1024]{3,2,1,0:T(8,128)} copy(f32[3,4,64,1024]{3,2,1,0:T(8,128)} %get-tuple-element.4) | data formatting | bytes 6291456
  48.1 0.0 copy-done
  48.1 0.6 %copy.9 = f32[2,64,64]{2,1,0:T(8,128)} copy(f32[2,64,64]{2,1,0:T(8,128)S(1)} %copy-done) | data formatting | bytes 65536
Async XLA Ops:
  44.1 4.0 %copy-start = (f32[2,64,64]{2,1,0:T(8,128)S(1)}, f32[2,64,64]{2,1,0:T(8,128)}, u32[]{:S(2)}) copy-start(f32[2,64,64]{2,1,0:T(8,128)} %get-tuple-element.5) | copy-start | bytes 98308

commit v6 on v5

--- a/solution.py
+++ b/solution.py
@@ -31,7 +31,7 @@
 LOCAL = 4
 VMEM_LIMIT = 63 * 1024 * 1024
 RING = 4
-CHUNKS = 2
+CHUNKS = 1
 PIECE = ROWS // CHUNKS
 PACKED = 72
 EDGE = 12 * 3 + 1
@@ -453,11 +453,11 @@
         tile = (Q[j, y] + Y_in[j, 0]) + (Y_in[j, 1] + Y_in[j, 2])
         T[j] = tile
         ends = (0, s_up, T.at[j, ROWS - 8 : ROWS]), (1, s_down, T.at[j, 0:8])
+        if j < 3:
+            send(("sum", j), T.at[j], Z_in.at[j], owner, s)
         for b, to_s, rows in ends:
             for a, to_f in neighbours:
                 send(("corner", a, b, j), rows, K_in.at[a, b, j], to_f, to_s)
-        if j < 3:
-            send(("sum", j), T.at[j], Z_in.at[j], owner, s)
         for b, to_s, rows in ends:
             send(("end", b, j), rows, E_in.at[b, j], owner, to_s)
         for (a, to_f), edge in zip(neighbours, edges(tile)):

time: 48.8 us -> 48.1 us (0.986)
  Pallas kernels: 43.4 us -> 42.7 us
    pallas_call x1, Pallas kernels: 43.4 us -> 42.7 us  [per_device(): pl.pallas_call(kernel, out_shape=(jax.ShapeDtypeStruct(fields.shape, F32)...]
where the time goes in v6:
time: 48.1 us; the launch traced here: 48 us
  Pallas kernels  42.7 us (89%)
  local copies, waits for them, and re-layouts  4.63 us (10%)
  between operations  0.65 us (1%)
    pallas_call x1, Pallas kernels, per_device(): pl.pallas_call(kernel, out_shape=(jax.ShapeDtypeStruct(fields.shape, F32)...  42.7 us
    unnamed x4, local copies, waits for them, and re-layouts  4.63 us

profile of v6, /device:TPU:1, one launch (start us, length us, event | category | flops | bytes accessed | tf_op | source)
XLA Modules:
  0.0 48.0 jit_solution(1216889464491165467)
XLA Ops:
  0.6 42.7 %step.1 = (f32[3,4,64,1024]{3,2,1,0:T(8,128)}, f32[2,64,64]{2,1,0:T(8,128)}) custom-call(f32[3,4,64,1024]{3,2,1,0:T(8,128)} %fields.1, f32[3,4,64,1024]{3,2,1,0:T(8,128)} %noise.1, f32[2,64,64]{2,1,0:T(8,128)} %velocity.1, s32[64,1024]{1,0:T(8,128)} %geometry.1), custom_call_target="tpu_custom_call" | custom-call | tf_op jit(solution)/shard_map/step/pallas_call | solution.py:583
  43.3 0.0 copy-start
  43.3 4.0 %copy.8 = f32[3,4,64,1024]{3,2,1,0:T(8,128)} copy(f32[3,4,64,1024]{3,2,1,0:T(8,128)} %get-tuple-element.4) | data formatting | bytes 6291456
  47.3 0.0 copy-done
  47.3 0.6 %copy.9 = f32[2,64,64]{2,1,0:T(8,128)} copy(f32[2,64,64]{2,1,0:T(8,128)S(1)} %copy-done) | data formatting | bytes 65536
Async XLA Ops:
  43.3 4.0 %copy-start = (f32[2,64,64]{2,1,0:T(8,128)S(1)}, f32[2,64,64]{2,1,0:T(8,128)}, u32[]{:S(2)}) copy-start(f32[2,64,64]{2,1,0:T(8,128)} %get-tuple-element.5) | copy-start | bytes 98308

commit v7 on v6

--- a/solution.py
+++ b/solution.py
@@ -158,29 +158,8 @@
     VR_out[0, 0:8, :] = own[ROWS - 8 :]
     VR_out[1, 0:8, :] = own[0:8]
 
-    load_g.wait()
-    half = f % 2
-    t_own = f // 2
-
-    def walls(rows):
-        def block(t):
-            at = pl.multiple_of(jnp.clip(t, 0, COLS - 1) * LANES, LANES)
-            return G[rows, pl.ds(at, LANES)].astype(F32)
-
-        before, here, after = block(t_own - 1), block(t_own), block(t_own + 1)
-        count = here.shape[0]
-        at = lax.broadcasted_iota(jnp.int32, (count, LANES), 1)
-        even = pltpu.roll(jnp.where(at < 120, here, before), HALO, axis=1)
-        odd = pltpu.roll(jnp.where(at < HALO, after, here), HALO + TILE, axis=1)
-        return jnp.where(half == 0, even, odd)
-
-    VR_out[0, 8:16, :] = walls(slice(ROWS - 8, ROWS))
-    VR_out[1, 8:16, :] = walls(slice(0, 8))
-
     pl.semaphore_wait(barrier, len(partners))
 
-    send(("vrow", 0), VR_out.at[0], VR_in.at[0], f, s_up)
-    send(("vrow", 1), VR_out.at[1], VR_in.at[1], f, s_down)
     for d in range(1, TILES):
         send(("max", d), M_own, M_all.at[d], f, (s + d) % TILES)
     main = PG.at[f, 0:ROWS]
@@ -190,6 +169,28 @@
             send(("z", o, h), piece, piece, z_peer(o), s)
     for d in (2, 1, 3):
         send(("y", d), main, main, y_peer(d), s)
+
+    load_g.wait()
+    half = f % 2
+    t_own = f // 2
+
+    def walls(rows):
+        def block(t):
+            at = pl.multiple_of(jnp.clip(t, 0, COLS - 1) * LANES, LANES)
+            return G[rows, pl.ds(at, LANES)].astype(F32)
+
+        before, here, after = block(t_own - 1), block(t_own), block(t_own + 1)
+        count = here.shape[0]
+        at = lax.broadcasted_iota(jnp.int32, (count, LANES), 1)
+        even = pltpu.roll(jnp.where(at < 120, here, before), HALO, axis=1)
+        odd = pltpu.roll(jnp.where(at < HALO, after, here), HALO + TILE, axis=1)
+        return jnp.where(half == 0, even, odd)
+
+    VR_out[0, 8:16, :] = walls(slice(ROWS - 8, ROWS))
+    VR_out[1, 8:16, :] = walls(slice(0, 8))
+
+    send(("vrow", 0), VR_out.at[0], VR_in.at[0], f, s_up)
+    send(("vrow", 1), VR_out.at[1], VR_in.at[1], f, s_down)
 
     for copy in loads:
         copy.wait()

time: 48.1 us -> 48.2 us (level)
  no operation moved by 1% of the time
where the time goes in v7:
time: 48.2 us; the launch traced here: 48.1 us
  Pallas kernels  42.8 us (89%)
  local copies, waits for them, and re-layouts  4.63 us (10%)
  between operations  0.65 us (1%)
    pallas_call x1, Pallas kernels, per_device(): pl.pallas_call(kernel, out_shape=(jax.ShapeDtypeStruct(fields.shape, F32)...  42.8 us
    unnamed x4, local copies, waits for them, and re-layouts  4.63 us

profile of v7, /device:TPU:1, one launch (start us, length us, event | category | flops | bytes accessed | tf_op | source)
XLA Modules:
  0.0 48.1 jit_solution(8167217728715317335)
XLA Ops:
  0.6 42.8 %step.1 = (f32[3,4,64,1024]{3,2,1,0:T(8,128)}, f32[2,64,64]{2,1,0:T(8,128)}) custom-call(f32[3,4,64,1024]{3,2,1,0:T(8,128)} %fields.1, f32[3,4,64,1024]{3,2,1,0:T(8,128)} %noise.1, f32[2,64,64]{2,1,0:T(8,128)} %velocity.1, s32[64,1024]{1,0:T(8,128)} %geometry.1), custom_call_target="tpu_custom_call" | custom-call | tf_op jit(solution)/shard_map/step/pallas_call | solution.py:584
  43.5 0.0 copy-start
  43.5 4.0 %copy.8 = f32[3,4,64,1024]{3,2,1,0:T(8,128)} copy(f32[3,4,64,1024]{3,2,1,0:T(8,128)} %get-tuple-element.4) | data formatting | bytes 6291456
  47.5 0.0 copy-done
  47.5 0.6 %copy.9 = f32[2,64,64]{2,1,0:T(8,128)} copy(f32[2,64,64]{2,1,0:T(8,128)S(1)} %copy-done) | data formatting | bytes 65536
Async XLA Ops:
  43.5 4.0 %copy-start = (f32[2,64,64]{2,1,0:T(8,128)S(1)}, f32[2,64,64]{2,1,0:T(8,128)}, u32[]{:S(2)}) copy-start(f32[2,64,64]{2,1,0:T(8,128)} %get-tuple-element.5) | copy-start | bytes 98308
